TPU v7x, 32 devices: a whole 2x2x4 slice. The times are simulated.
32 devices in a mesh: dist: 4 (over x, core), ctr: 8 (over z, y).
Axes of the slice: x: 2, y: 2, z: 4, core: 2. Of those that a mesh axis runs over, the one named last changes fastest.
Arguments:
- three_centre: bfloat16 [1024, 4, 4096], P(('dist', 'ctr')), may hold values from -0.359375 to 0.359375
- occupied_green: bfloat16 [128, 4096], P(('dist', 'ctr')), may hold values from -0.75 to 0.75
- virtual_green: bfloat16 [128, 4096], P(('dist', 'ctr')), may hold values from -0.75 to 0.75
- pair_index: int32 [16, 4], replicated, may hold values from 0 to 7, as said below
- source_slot: int32 [16, 4, 4], replicated, may hold values from -1 to 3, as said below
- occupied_index: int32 [16, 4, 4], replicated, may hold values from 0 to 127, as said below
- virtual_index: int32 [16, 4, 4], replicated, may hold values from 0 to 127, as said below
Outputs:
- density_response: float32 [1024, 256], P(('dist', 'ctr'))
Inputs may be any that keep to these rules, and one draw needn't show every extreme that they name: `pair_index`: the 4 entries of a row are distinct. `source_slot`: for each slot the listed slots are distinct and come first, followed by -1 entries; all slots of one auxiliary atom list the same number of slots, at least 1; in every draw some auxiliary atom lists 4. `occupied_index`: for auxiliary atom p with g = p // 4, every entry lies in g * 32 to g * 32 + 2 * 32 - 1, taken modulo 128. `virtual_index`: for auxiliary atom p with g = p // 4, every entry lies in g * 32 to g * 32 + 2 * 32 - 1, taken modulo 128.
All inputs are finite; a program needn't handle non-finite values.
Results may differ from a plain program's by a relative error of at most 0.004.
Values may be sent and summed in bfloat16 or wider, within the bound.
A program may use at most 64 MiB of HBM per device.

v0:
```python
import functools

import jax
import jax.numpy as jnp
from jax import lax
from jax.experimental import pallas as pl
from jax.experimental.pallas import tpu as pltpu
from jax.sharding import PartitionSpec as P

BLK = 64
NPR = 8
LANES = 128
F32 = jnp.float32
BF16 = jnp.bfloat16


def kernel(n, groups, atoms, ids, t_ref, green_ref, out_ref, table, tf, tt, wcat, ocat, usend, urecv, trecv,
           uk, tk, part, psend, precv, g_send, g_recv, t_send, t_recv, u_send, u_recv, p_send, p_recv, own_sem):
    slots, rows, width = t_ref.shape
    chunks = width // LANES
    blocks = green_ref.shape[0] // 2
    cols = width // n
    per = cols // LANES
    dist = lax.axis_index("dist")
    me = lax.axis_index("ctr")
    before = lax.rem(dist + groups - 1, groups)
    after = lax.rem(dist + 1, groups)

    far_first = sorted(range(1, n), key=lambda k: -min(k, n - k))

    def ahead(k):
        return lax.rem(me + k, n)

    def signal(d, c):
        pl.semaphore_signal(barrier, inc=1, device_id=(d, c), device_id_type=pl.DeviceIdType.MESH)

    def remote(src, dst, send, recv, d, c):
        return pltpu.make_async_remote_copy(
            src_ref=src, dst_ref=dst, send_sem=send, recv_sem=recv, device_id=(d, c),
            device_id_type=pl.DeviceIdType.MESH,
        )

    barrier = pltpu.get_barrier_semaphore()
    for k in range(1, n):
        signal(dist, ahead(k))
    signal(before, me)
    signal(after, me)

    row = lax.broadcasted_iota(jnp.int32, (BLK, BLK), 0)
    col = lax.broadcasted_iota(jnp.int32, (BLK, BLK), 1)
    half = BLK // 2
    wanted = jnp.where(row < half, 2 * row, 2 * (row - half) + 1)
    perm = (wanted == col).astype(BF16)
    mine = me * blocks
    for b in range(blocks):
        occ = green_ref[blocks + b]
        turned = lax.dot_general(perm, occ, (((1,), (1,)), ((), ())), preferred_element_type=F32).astype(BF16)
        turned = lax.dot_general(turned, perm, (((1,), (1,)), ((), ())), preferred_element_type=F32).astype(BF16)
        table[mine + b] = jnp.concatenate([green_ref[b], turned], axis=1)

    pl.semaphore_wait(barrier, n + 1)

    lines = n // 2
    high, low = me // 2, lax.rem(me, 2)
    partner = high * 2 + 1 - low

    def line(k):
        return lax.rem(high + k, lines) * 2

    def at_home(c):
        return table.at[pl.ds(c * blocks, blocks)]

    def across(c):
        return table.at[pl.ds((n + c) * blocks, blocks)]

    first_hop = [
        remote(at_home(me), at_home(me), g_send.at[0, k], g_recv.at[0, k], dist, line(k) + low)
        for k in range(1, lines)
    ]
    for copy in first_hop:
        copy.start()

    def t_part(c):
        return t_ref.at[:, :, pl.ds(pl.multiple_of(c * cols, LANES), cols)]

    tensor = [
        remote(t_part(ahead(k)), trecv.at[me], t_send.at[k], t_recv.at[k], dist, ahead(k)) for k in far_first
    ]
    for copy in tensor:
        copy.start()
    own_t = pltpu.make_async_copy(t_part(me), trecv.at[me], own_sem.at[0])
    own_t.start()

    second_hop, third_hop = [], []
    for k in range(lines):
        if k:
            first_hop[k - 1].wait_recv()
        c = line(lines - k) + low
        second_hop.append(remote(at_home(c), at_home(c), g_send.at[1, k], g_recv.at[1, k], dist, partner))
        second_hop[-1].start()
        third_hop.append(remote(at_home(c), across(c), g_send.at[2, k], g_recv.at[2, k], before, me))
        third_hop[-1].start()

    def turn(s, carry):
        for j in range(chunks):
            tf[j * rows:(j + 1) * rows, :] = t_ref[s, :, j * LANES:(j + 1) * LANES].astype(F32)
        for i in range(rows):
            tt[s, i * chunks:(i + 1) * chunks, :] = tf[pl.ds(i, chunks, stride=rows), :].astype(BF16)
        return carry

    lax.fori_loop(0, slots, turn, 0)

    for k in range(lines):
        second_hop[k].wait_recv()
        c = line(lines - k) + 1 - low
        third_hop.append(remote(at_home(c), across(c), g_send.at[3, k], g_recv.at[3, k], before, me))
        third_hop[-1].start()
    for copy in third_hop:
        copy.wait()
    for copy in first_hop + second_hop:
        copy.wait_send()

    size = atoms * slots
    atom = (dist * n + me) * rows // BLK
    total = n * blocks * groups
    base = dist * n * blocks

    def position(value):
        shift = value - base
        return jnp.minimum(jnp.where(shift < 0, shift + total, shift), 2 * n * blocks - 1)

    step_rows = 8 * chunks
    lane = lax.broadcasted_iota(jnp.int32, (half, LANES), 1)

    def update(s, carry):
        at = (atom * slots + s) * slots
        for r in range(slots):
            src = ids[at + r]
            live = jnp.where(src >= 0, 1.0, 0.0).astype(F32)
            src = jnp.maximum(src, 0)
            virt = table[position(ids[2 * size * slots + at + r])].astype(F32)[:, :BLK] * live
            zero = jnp.zeros((BLK, LANES), F32)
            twice = jnp.concatenate([virt, virt], axis=1)
            weight = jnp.concatenate(
                [jnp.concatenate([twice, zero], axis=1), jnp.concatenate([zero, twice], axis=1)], axis=0
            ).astype(BF16)
            ocat[:, r * BLK:(r + 1) * BLK] = table[position(ids[size * slots + at + r])][:, BLK:]
            for h in range(rows // 8):
                got = jnp.dot(
                    tt[src, h * step_rows:(h + 1) * step_rows, :], weight, preferred_element_type=F32
                ).astype(BF16)
                for x in range(8):
                    i = h * 8 + x
                    for e in range(2):
                        wcat[r * BLK + e * half:r * BLK + (e + 1) * half, i * LANES:(i + 1) * LANES] = got[
                            x * chunks:(x + 1) * chunks, e * LANES:(e + 1) * LANES
                        ]
        occ = ocat[...]
        for h in range(rows // 4):
            both = jnp.dot(occ, wcat[:, h * 4 * LANES:(h + 1) * 4 * LANES], preferred_element_type=F32)
            for x in range(4):
                i = h * 4 + x
                piece = both[:, x * LANES:(x + 1) * LANES]
                tf[i * chunks:(i + 1) * chunks, :] = jnp.where(lane < BLK, piece[:half], piece[half:])
        for q in range(chunks):
            usend[s, q // per, :, (q % per) * LANES:(q % per + 1) * LANES] = tf[
                pl.ds(q, rows, stride=chunks), :
            ].astype(BF16)
        for k in far_first:
            sent(s, k).start()
        return carry

    def sent(s, k):
        return remote(
            usend.at[s, ahead(k)], urecv.at[me, s], u_send.at[s, k], u_recv.at[s, k], dist, ahead(k)
        )

    lax.fori_loop(0, slots, update, 0)
    own_u = pltpu.make_async_copy(usend.at[:, me], urecv.at[me], own_sem.at[1])
    own_u.start()
    own_t.wait()
    for copy in tensor:
        copy.wait()

    first = dist * (n * rows // BLK)
    pairs = 3 * size * slots

    def pick(src, pair, p):
        where = pairs + (first + p * rows // BLK) * slots
        slot = jnp.int32(0)
        live = jnp.int32(0)
        for s in range(slots):
            hit = ids[where + s] == pair
            slot = jnp.where(hit, s, slot)
            live = jnp.where(hit, 1, live)
        return (src[p, slot].astype(F32) * live.astype(F32)).astype(BF16)

    def at_rows(p):
        return pl.ds(pl.multiple_of(p * rows, rows), rows)

    def at_cols(pair):
        return pl.ds(pl.multiple_of(pair * cols, LANES), cols)

    def tensor_pair(pair, carry):
        def gather(p, inner):
            tk[at_rows(p), at_cols(pair)] = pick(trecv, pair, p)
            return inner

        return lax.fori_loop(0, n, gather, carry)

    lax.fori_loop(0, NPR, tensor_pair, 0)

    def updated_pairs(p):
        where = pairs + (first + p * rows // BLK) * slots

        def one_pair(pair, carry):
            chosen = jnp.zeros((rows, cols), F32)
            for s in range(slots):
                hit = jnp.where(ids[where + s] == pair, 1.0, 0.0).astype(F32)
                chosen = chosen + urecv[p, s].astype(F32) * hit
            uk[at_rows(p), at_cols(pair)] = chosen.astype(BF16)
            return carry

        lax.fori_loop(0, NPR, one_pair, 0)

    own_u.wait()
    updated_pairs(me)
    for k in far_first[::-1]:
        for s in range(slots):
            sent(s, k).wait()
        updated_pairs(lax.rem(me - k + n, n))

    def block(p, carry):
        at = pl.ds(pl.multiple_of(p * 256, 256), 256)
        total = lax.dot_general(uk[at, :], tk[...], (((1,), (1,)), ((), ())), preferred_element_type=F32)
        part[at, :] = total
        psend[at, :] = total.astype(BF16)
        return carry

    lax.fori_loop(0, n * rows // 256, block, 0)

    def p_part(c):
        return psend.at[pl.ds(pl.multiple_of(c * rows, rows), rows)]

    shares = [
        remote(p_part(ahead(k)), precv.at[k], p_send.at[k], p_recv.at[k], dist, ahead(k)) for k in far_first
    ]
    for copy in shares:
        copy.start()
    result = part[pl.ds(pl.multiple_of(me * rows, rows), rows), :]
    for k, copy in zip(far_first, shares):
        copy.wait()
        result = result + precv[k].astype(F32)
    out_ref[...] = result


def solution(mesh):
    n = mesh.shape["ctr"]
    groups = mesh.shape["dist"]

    def shards(three_centre, occupied_green, virtual_green, pair_index, source_slot, occupied_index, virtual_index):
        rows, slots, width = three_centre.shape
        blocks = occupied_green.shape[0]
        atoms = pair_index.shape[0]
        chunks = width // LANES
        cols = width // n
        tensor = jnp.transpose(three_centre, (1, 0, 2))
        green = jnp.concatenate([virtual_green, occupied_green], axis=0).reshape(2 * blocks, BLK, BLK)
        ids = jnp.concatenate(
            [x.reshape(-1) for x in (source_slot, occupied_index, virtual_index, pair_index)]
        )
        vmem = pl.BlockSpec(memory_space=pltpu.VMEM)
        dma = pltpu.SemaphoreType.DMA
        return pl.pallas_call(
            functools.partial(kernel, n, groups, atoms),
            out_shape=jax.ShapeDtypeStruct((rows, n * rows), F32),
            in_specs=[pl.BlockSpec(memory_space=pltpu.SMEM), vmem, vmem],
            out_specs=vmem,
            scratch_shapes=[
                pltpu.VMEM((2 * n * blocks, BLK, LANES), BF16),
                pltpu.VMEM((rows * chunks, LANES), F32),
                pltpu.VMEM((slots, rows * chunks, LANES), BF16),
                pltpu.VMEM((slots * BLK, rows * LANES), BF16),
                pltpu.VMEM((BLK, slots * BLK), BF16),
                pltpu.VMEM((slots, n, rows, cols), BF16),
                pltpu.VMEM((n, slots, rows, cols), BF16),
                pltpu.VMEM((n, slots, rows, cols), BF16),
                pltpu.VMEM((n * rows, NPR * cols), BF16),
                pltpu.VMEM((n * rows, NPR * cols), BF16),
                pltpu.VMEM((n * rows, n * rows), F32),
                pltpu.VMEM((n * rows, n * rows), BF16),
                pltpu.VMEM((n, rows, n * rows), BF16),
                dma((4, n // 2)),
                dma((4, n // 2)),
                dma((n,)),
                dma((n,)),
                dma((slots, n)),
                dma((slots, n)),
                dma((n,)),
                dma((n,)),
                dma((2,)),
            ],
            compiler_params=pltpu.CompilerParams(
                collective_id=0, has_side_effects=True, vmem_limit_bytes=48 * 2**20
            ),
        )(ids, tensor, green)

    return jax.shard_map(
        shards,
        mesh=mesh,
        in_specs=(
            P(("dist", "ctr"), None, None),
            P(("dist", "ctr"), None),
            P(("dist", "ctr"), None),
            P(),
            P(),
            P(),
            P(),
        ),
        out_specs=P(("dist", "ctr"), None),
        check_vma=False,
    )
```

profile of v0, /device:TPU:0, one launch (start us, length us, event | category | flops | bytes accessed | tf_op | source)
XLA Modules:
  0.0 72.3 jit_solution(16890440151395129961)
XLA Ops:
  0.0 0.0 copy-start.2
  0.0 0.8 %copy.13 = s32[16,4]{1,0:T(8,128)S(1)} copy(s32[16,4]{0,1:T(4,128)} %param.10) | data formatting | bytes 512 | tf_op args[3]
  0.8 0.1 reshape.18
  0.9 0.0 copy-done.2
  0.9 0.1 copy.10
  1.0 0.0 copy-start.3
  1.0 0.1 reshape.15
  1.1 0.6 copy-done.3
  1.7 0.1 copy.11
  1.8 0.0 copy-start.4
  1.8 0.1 reshape.16
  1.9 0.6 copy-done.4
  2.5 0.0 copy-start
  2.5 0.0 copy-start.1
  2.5 0.1 copy.12
  2.6 0.1 reshape.17
  2.7 0.5 copy-done
  3.2 0.0 copy-done.1
  3.3 0.2 reshape.19.green_ref
  3.5 1.8 %copy.16 = bf16[32,4,4096]{2,0,1:T(8,128)(2,1)S(1)} copy(bf16[32,4,4096]{2,1,0:T(4,128)(2,1)} %param.7) | data formatting | bytes 2097152 | tf_op args[0]
  5.3 66.4 %shard_map.73 = f32[32,256]{1,0:T(8,128)S(1)} custom-call(s32[832]{0:T(1024)S(1)} %pad_add_fusion.ids, bf16[4,32,4096]{2,1,0:T(8,128)(2,1)S(1)} %bitcast.3, bf16[8,64,64]{2,1,0:T(8,128)(2,1)S(1)} %reshape.19.green_ref), custom_call_target="tpu_custom_call" | custom-call | tf_op jit(solution)/shard_map/pallas_call | solution.py:274
  71.7 0.6 copy.18
  (2 shorter events, 0.0 us)
Async XLA Ops:
  0.0 0.9 %copy-start.2 = (s32[16,4,4]{0,2,1:T(4,128)S(1)}, s32[16,4,4]{0,2,1:T(4,128)}, u32[]{:S(2)}) copy-start(s32[16,4,4]{0,2,1:T(4,128)} %param.11) | copy-start | bytes 3076
  1.0 0.7 copy-start.3
  1.8 0.7 copy-start.4
  2.5 0.8 %copy-start = (bf16[4,4096]{1,0:T(4,128)(2,1)S(1)}, bf16[4,4096]{1,0:T(4,128)(2,1)}, u32[]{:S(2)}) copy-start(bf16[4,4096]{1,0:T(4,128)(2,1)} %param.8) | copy-start | bytes 98308
  2.5 0.8 %copy-start.1 = (bf16[4,4096]{1,0:T(4,128)(2,1)S(1)}, bf16[4,4096]{1,0:T(4,128)(2,1)}, u32[]{:S(2)}) copy-start(bf16[4,4096]{1,0:T(4,128)(2,1)} %param.9) | copy-start | bytes 98308
where the time goes:
time: 72.7 us; the launch traced here: 72.3 us
  Pallas kernels  66.4 us (91%)
  local copies, waits for them, and re-layouts  5.81 us (8%)
    pallas_call x1, Pallas kernels, shards(): pl.pallas_call(functools.partial(kernel, n, groups, atoms), out_shape=jax...  66.4 us
    unnamed x16, local copies, waits for them, and re-layouts  5.22 us

commit v1 on v0

--- a/solution.py
+++ b/solution.py
@@ -254,6 +254,446 @@
     out_ref[...] = result
 
 
+def iota(shape, dim):
+    return lax.broadcasted_iota(jnp.int32, shape, dim)
+
+
+def nt(a, b):
+    return lax.dot_general(a, b, (((1,), (1,)), ((), ())), preferred_element_type=F32)
+
+
+def nn(a, b):
+    return jnp.dot(a, b, preferred_element_type=F32)
+
+
+def line_kernel(n, groups, atoms, ids, t_ref, green_ref, out_ref, table, halves, moved, stack, swapped, tf, xg, wg, uf,
+                first_op, second_op, gather, select, place, lift, turn_v, blk, cross, partner_in, cross_in,
+                g_send, g_recv, y_send, y_recv, m_send, m_recv, c_send, c_recv, p_send, p_recv):
+    slots, rows, width = t_ref.shape
+    blocks = green_ref.shape[0] // 2
+    chunks = width // LANES
+    half = BLK // 2
+    part_rows = rows // 2
+    deep = BLK * LANES
+    dist = lax.axis_index("dist")
+    me = lax.axis_index("ctr")
+    before = lax.rem(dist + groups - 1, groups)
+    after = lax.rem(dist + 1, groups)
+    lines = n // 2
+    high, low = me // 2, lax.rem(me, 2)
+    partner = high * 2 + 1 - low
+    mirrored = lax.rem(dist, 2)
+
+    def flip(a):
+        return jnp.where(mirrored == 1, lines - 1 - a, a)
+
+    place_at = flip(high)
+
+    def at_place(a, y):
+        return flip(a) * 2 + y
+
+    def signal(d, c):
+        pl.semaphore_signal(barrier, inc=1, device_id=(d, c), device_id_type=pl.DeviceIdType.MESH)
+
+    def remote(src, dst, send, recv, d, c):
+        return pltpu.make_async_remote_copy(
+            src_ref=src, dst_ref=dst, send_sem=send, recv_sem=recv, device_id=(d, c),
+            device_id_type=pl.DeviceIdType.MESH,
+        )
+
+    barrier = pltpu.get_barrier_semaphore()
+    for k in range(1, n):
+        signal(dist, lax.rem(me + k, n))
+    signal(before, me)
+    signal(after, me)
+
+    row, col = iota((BLK, BLK), 0), iota((BLK, BLK), 1)
+    wanted = jnp.where(row < half, 2 * row, 2 * (row - half) + 1)
+    perm = (wanted == col).astype(BF16)
+    mine = me * blocks
+    for b in range(blocks):
+        turned = nn(perm, green_ref[blocks + b]).astype(BF16)
+        turned = nt(turned, perm).astype(BF16)
+        table[mine + b] = jnp.concatenate([green_ref[b], turned], axis=1)
+
+    wide = slots * LANES
+    r_, c_ = iota((wide, wide), 0), iota((wide, wide), 1)
+    select[...] = (
+        r_ == ((c_ // half) % slots) * LANES + ((c_ // LANES) % 2) * BLK + (c_ // (2 * LANES)) * half + c_ % half
+    ).astype(BF16)
+    r_, c_ = iota((wide, slots * BLK), 0), iota((wide, slots * BLK), 1)
+    place[...] = ((r_ % LANES >= BLK) & (c_ == (r_ // LANES) * BLK + r_ % LANES - BLK)).astype(BF16)
+    r_, c_ = iota((2 * LANES, LANES), 0), iota((2 * LANES, LANES), 1)
+    for t in range(slots):
+        lift[t] = ((c_ < BLK) & (r_ == (c_ // half) * LANES + t * half + c_ % half)).astype(BF16)
+    r_, c_ = iota((LANES, wide), 0), iota((LANES, wide), 1)
+    turn_v[...] = ((r_ // half == c_ // LANES) & (c_ % LANES == low * half + r_ % half)).astype(BF16)
+
+    own_rows = pl.ds(pl.multiple_of(low * rows, rows), rows)
+    per = 8
+    for q in range(0, chunks, per):
+        x = jnp.concatenate(
+            [
+                jnp.concatenate([t_ref[j, :, (q + p) * LANES:(q + p + 1) * LANES] for j in range(slots)], axis=1)
+                for p in range(per)
+            ],
+            axis=0,
+        )
+        got = nn(x, select[...]).astype(BF16)
+        for p in range(per):
+            for h in range(2):
+                for e in range(2):
+                    at = (e * half + q + p) * LANES
+                    halves[h, own_rows, at:at + LANES] = got[
+                        p * rows:(p + 1) * rows, (h * 2 + e) * LANES:(h * 2 + e + 1) * LANES
+                    ]
+
+    pl.semaphore_wait(barrier, n + 1)
+
+    def line(k):
+        return lax.rem(high + k, lines) * 2
+
+    def at_home(c):
+        return table.at[pl.ds(c * blocks, blocks)]
+
+    def across(c):
+        return table.at[pl.ds((n + c) * blocks, blocks)]
+
+    first_hop = [
+        remote(at_home(me), at_home(me), g_send.at[0, k], g_recv.at[0, k], dist, line(k) + low)
+        for k in range(1, lines)
+    ]
+    for copy in first_hop:
+        copy.start()
+
+    def rows_of(k):
+        y = low if k < 2 else 1 - low
+        return pl.ds(pl.multiple_of(y * rows + (k % 2) * part_rows, part_rows), part_rows)
+
+    def over_y(phase, k):
+        h = 1 - low if phase == 0 else low
+        at = halves.at[h, rows_of(k)]
+        return remote(at, at, y_send.at[phase, k], y_recv.at[phase, k], dist, partner)
+
+    def from_y(phase, k):
+        at = halves.at[low if phase == 0 else 1 - low, rows_of(2 + k)]
+        return remote(at, at, y_send.at[phase, k], y_recv.at[phase, k], dist, partner)
+
+    pieces = 2
+    piece = deep // pieces
+
+    def over_z(slot, k, x, own, to):
+        at, lanes = rows_of(k), pl.ds(x * piece, piece)
+        src = halves.at[low, at, lanes] if own else moved.at[slot, at, lanes]
+        sem = k * pieces + x
+        return remote(
+            src, moved.at[slot, at, lanes], m_send.at[slot, sem], m_recv.at[slot, sem], dist, at_place(to, low)
+        )
+
+    starts = {0: (0, 1), 1: (1, 2), 3: (2, 2)}
+
+    def send_own(k):
+        for a, (slot, to) in starts.items():
+            @pl.when(place_at == a)
+            def _():
+                for x in range(pieces):
+                    over_z(slot, k, x, True, to).start()
+
+    over_y(0, 0).start()
+    for k in range(2):
+        send_own(k)
+    second_hop, third_hop = [], []
+    for k in range(lines):
+        if k:
+            first_hop[k - 1].wait_recv()
+        c = line(lines - k) + low
+        second_hop.append(remote(at_home(c), at_home(c), g_send.at[1, k], g_recv.at[1, k], dist, partner))
+        second_hop[-1].start()
+        third_hop.append(remote(at_home(c), across(c), g_send.at[2, k], g_recv.at[2, k], before, me))
+        third_hop[-1].start()
+    over_y(0, 1).start()
+
+    def relay(slot, k):
+        for a in {0: (1, 2), 1: (2,), 2: ()}[slot]:
+            @pl.when(place_at == a)
+            def _():
+                for x in range(pieces):
+                    over_z(slot, k, x, False, a).wait_recv()
+                    over_z(slot, k, x, False, a + 1).start()
+
+    relay(1, 0)
+    relay(0, 0)
+    from_y(0, 0).wait_recv()
+    send_own(2)
+    relay(1, 1)
+    relay(0, 1)
+
+    for k in range(lines):
+        second_hop[k].wait_recv()
+        c = line(lines - k) + 1 - low
+        third_hop.append(remote(at_home(c), across(c), g_send.at[3, k], g_recv.at[3, k], before, me))
+        third_hop[-1].start()
+
+    from_y(0, 1).wait_recv()
+    send_own(3)
+    for k in range(2):
+        over_y(0, k).wait_send()
+        over_y(1, k).start()
+    for copy in third_hop:
+        copy.wait()
+    for copy in first_hop + second_hop:
+        copy.wait_send()
+    relay(1, 2)
+    relay(0, 2)
+
+    size = atoms * slots
+    occ_at, virt_at, pair_at = size * slots, 2 * size * slots, 3 * size * slots
+    total = n * blocks * groups
+    base = dist * n * blocks
+    atom = dist * lines + high
+
+    def position(value):
+        shift = value - base
+        return jnp.minimum(jnp.where(shift < 0, shift + total, shift), 2 * n * blocks - 1)
+
+    def atom_at(a):
+        return dist * lines + flip(a)
+
+    def feeding(a, s, j):
+        r, live = jnp.int32(0), jnp.int32(0)
+        for x in range(slots):
+            hit = ids[(a * slots + s) * slots + x] == j
+            r, live = jnp.where(hit, x, r), jnp.where(hit, 1, live)
+        return r, live
+
+    def green(a, s, r, live):
+        at = (a * slots + s) * slots + r
+        return position(ids[occ_at + at]), position(ids[virt_at + at]), live.astype(F32)
+
+    for t in range(slots):
+        virt = []
+        for o in range(slots):
+            r, live = feeding(atom, o, t)
+            occ_pos, virt_pos, live = green(atom, o, r, live)
+            virt.append((table[virt_pos].astype(F32) * live).astype(BF16))
+            gather[t * BLK:(t + 1) * BLK, o * LANES:(o + 1) * LANES] = table[occ_pos]
+        b = nt(turn_v[...], jnp.concatenate(virt, axis=1)).astype(BF16)
+        second_op[0, :, t * LANES:(t + 1) * LANES] = nt(lift[t][:, :BLK], b).astype(BF16)
+    size_op = slots * BLK
+    unit = (iota((size_op, size_op), 0) == iota((size_op, size_op), 1)).astype(BF16)
+    first_op[0] = nt(unit, nn(gather[...], place[...]).astype(BF16)).astype(BF16)
+
+    def operators(slot, a):
+        other = atom_at(a)
+        for t in range(slots):
+            pair = ids[pair_at + atom * slots + t]
+            s, met = jnp.int32(0), jnp.int32(0)
+            for x in range(slots):
+                hit = ids[pair_at + other * slots + x] == pair
+                s, met = jnp.where(hit, x, s), jnp.where(hit, 1, met)
+            virt = []
+            for o in range(slots):
+                r, live = feeding(other, s, o)
+                occ_pos, virt_pos, live = green(other, s, r, live * met)
+                virt.append(
+                    (table[virt_pos, pl.ds(pl.multiple_of(low * half, half), half), :].astype(F32) * live).astype(BF16)
+                )
+                gather[o * BLK:(o + 1) * BLK, t * LANES:(t + 1) * LANES] = table[occ_pos]
+            second_op[1 + slot, :, t * LANES:(t + 1) * LANES] = nt(lift[t], jnp.concatenate(virt, axis=0)).astype(BF16)
+        first_op[1 + slot] = nn(gather[...], place[...]).astype(BF16)
+
+    used = {0: (0, (1, 2, 3)), 1: (1, (2, 3)), 2: (3, (2,))}
+
+    def wanted_here(slot):
+        hit = place_at == used[slot][1][0]
+        for a in used[slot][1][1:]:
+            hit = hit | (place_at == a)
+        return hit
+
+    for slot in used:
+        @pl.when(wanted_here(slot))
+        def _():
+            operators(slot, used[slot][0])
+
+    lanes2 = (iota((BLK, 2 * LANES), 1) // half) % slots
+
+    def one_stack(k, at_rows):
+        got = nn(xg[...], second_op[k]).astype(BF16)
+        for i in range(part_rows):
+            for t in range(slots):
+                wg[i, t * BLK:(t + 1) * BLK, :] = got[i * BLK:(i + 1) * BLK, t * LANES:(t + 1) * LANES]
+        for p in range(part_rows // 2):
+            both = nn(first_op[k], jnp.concatenate([wg[2 * p], wg[2 * p + 1]], axis=1))
+            res = both[:BLK]
+            for o in range(1, slots):
+                res = jnp.where(lanes2 == o, both[o * BLK:(o + 1) * BLK], res)
+            for x in range(2):
+                uf[(2 * p + x) * BLK:(2 * p + x + 1) * BLK, :] = res[:, x * LANES:(x + 1) * LANES]
+        for m in range(BLK):
+            stack[k, at_rows, m * LANES:(m + 1) * LANES] = uf[pl.ds(m, part_rows, stride=BLK), :].astype(BF16)
+
+    def transform(g):
+        at_rows = rows_of(g)
+        for h in range(2):
+            for m in range(BLK):
+                tf[h, m * part_rows:(m + 1) * part_rows, :] = halves[h, at_rows, m * LANES:(m + 1) * LANES].astype(F32)
+            for i in range(part_rows):
+                xg[i * BLK:(i + 1) * BLK, h * LANES:(h + 1) * LANES] = tf[
+                    h, pl.ds(i, BLK, stride=part_rows), :
+                ].astype(BF16)
+
+        def each(k, carry):
+            hit = (k == 0) | ((k == 1) & wanted_here(0)) | ((k == 2) & wanted_here(1)) | ((k == 3) & wanted_here(2))
+
+            @pl.when(hit)
+            def _():
+                one_stack(k, at_rows)
+            return carry
+
+        lax.fori_loop(0, 1 + len(used), each, 0)
+
+    for g in range(4):
+        if g >= 2:
+            from_y(1, g - 2).wait_recv()
+        transform(g)
+        if g == 0:
+            relay(1, 3)
+            relay(0, 3)
+
+    for c in range(lines):
+        blk[c] = jnp.zeros((BLK, LANES), F32)
+
+    def lay(x):
+        return jnp.concatenate([x, jnp.zeros((BLK, LANES - BLK), F32)], axis=1)
+
+    blk[high] = lay(nt(stack[0], halves[low]))
+
+    def returned(slot, y):
+        a = used[slot][0]
+        return remote(
+            cross.at[slot, pl.ds(y * rows, rows)], cross_in.at[place_at, low], c_send.at[slot, y],
+            c_recv.at[place_at, low], dist, at_place(a, y),
+        )
+
+    def product(slot):
+        a = used[slot][0]
+        for k in range(4):
+            if slot == 2:
+                for x in range(pieces):
+                    over_z(slot, k, x, False, a).wait_recv()
+            else:
+                @pl.when(place_at == 3)
+                def _():
+                    for x in range(pieces):
+                        over_z(slot, k, x, False, a).wait_recv()
+        cross[slot] = lay(nt(moved[slot], stack[1 + slot]))
+        for y in range(2):
+            returned(slot, y).start()
+        other = atom_at(a)
+        r_, c_ = iota((LANES, LANES), 0), iota((LANES, LANES), 1)
+        match = jnp.zeros((LANES, LANES), F32)
+        for s in range(slots):
+            for t in range(slots):
+                hit = jnp.where(ids[pair_at + atom * slots + s] == ids[pair_at + other * slots + t], 1.0, 0.0)
+                match = jnp.where((r_ // half == s) & (c_ // half == t), hit.astype(F32), match)
+        match = jnp.where(r_ % half == c_ % half, match, 0.0).astype(BF16)
+        for m in range(0, BLK, 8):
+            x = jnp.concatenate([stack[0, :, (m + p) * LANES:(m + p + 1) * LANES] for p in range(8)], axis=0)
+            got = nn(x, match).astype(BF16)
+            for p in range(8):
+                swapped[:, (m + p) * LANES:(m + p + 1) * LANES] = got[p * BLK:(p + 1) * BLK]
+        blk[flip(a)] = lay(nt(swapped[...], moved[slot]))
+
+    for slot in (1, 0, 2):
+        @pl.when(wanted_here(slot))
+        def _():
+            product(slot)
+
+    other_rows = pl.ds(pl.multiple_of((1 - low) * rows, rows), rows)
+    to_partner = remote(blk.at[:, other_rows], partner_in, p_send.at[0], p_recv.at[0], dist, partner)
+    to_partner.start()
+
+    came = {1: (0,), 2: (0, 1, 3), 3: (0, 1)}
+    for src, takers in came.items():
+        for a in takers:
+            @pl.when(place_at == a)
+            def _():
+                for y in range(2):
+                    remote(
+                        cross.at[0, pl.ds(0, rows)], cross_in.at[src, y], c_send.at[0, 0], c_recv.at[src, y], dist, me
+                    ).wait_recv()
+                blk[flip(src), own_rows] = cross_in[src, 0] + cross_in[src, 1]
+    to_partner.wait()
+    tiles = [(blk[c, own_rows] + partner_in[c])[:, :BLK] for c in range(lines)]
+    out_ref[...] = jnp.concatenate(tiles, axis=1)
+
+    for k in range(2):
+        over_y(1, k).wait_send()
+    for slot, senders in {0: (0, 1, 2), 1: (1, 2), 2: (3,)}.items():
+        for a in senders:
+            @pl.when(place_at == a)
+            def _():
+                for k in range(4):
+                    for x in range(pieces):
+                        over_z(slot, k, x, False, 0).wait_send()
+
+        @pl.when(wanted_here(slot))
+        def _():
+            for y in range(2):
+                returned(slot, y).wait_send()
+
+
+def on_line(n, groups, atoms, ids, tensor, green):
+    slots, rows, width = tensor.shape
+    blocks = green.shape[0] // 2
+    lines = n // 2
+    deep = BLK * LANES
+    part_rows = rows // 2
+    vmem = pl.BlockSpec(memory_space=pltpu.VMEM)
+    dma = pltpu.SemaphoreType.DMA
+    return pl.pallas_call(
+        functools.partial(line_kernel, n, groups, atoms),
+        out_shape=jax.ShapeDtypeStruct((rows, lines * BLK), F32),
+        in_specs=[pl.BlockSpec(memory_space=pltpu.SMEM), vmem, vmem],
+        out_specs=vmem,
+        scratch_shapes=[
+            pltpu.VMEM((2 * n * blocks, BLK, LANES), BF16),
+            pltpu.VMEM((2, BLK, deep), BF16),
+            pltpu.VMEM((3, BLK, deep), BF16),
+            pltpu.VMEM((4, BLK, deep), BF16),
+            pltpu.VMEM((BLK, deep), BF16),
+            pltpu.VMEM((2, part_rows * BLK, LANES), F32),
+            pltpu.VMEM((part_rows * BLK, 2 * LANES), BF16),
+            pltpu.VMEM((part_rows, slots * BLK, LANES), BF16),
+            pltpu.VMEM((part_rows * BLK, LANES), F32),
+            pltpu.VMEM((4, slots * BLK, slots * BLK), BF16),
+            pltpu.VMEM((4, 2 * LANES, slots * LANES), BF16),
+            pltpu.VMEM((slots * BLK, slots * LANES), BF16),
+            pltpu.VMEM((slots * LANES, slots * LANES), BF16),
+            pltpu.VMEM((slots * LANES, slots * BLK), BF16),
+            pltpu.VMEM((slots, 2 * LANES, LANES), BF16),
+            pltpu.VMEM((LANES, slots * LANES), BF16),
+            pltpu.VMEM((lines, BLK, LANES), F32),
+            pltpu.VMEM((3, BLK, LANES), F32),
+            pltpu.VMEM((lines, rows, LANES), F32),
+            pltpu.VMEM((lines, 2, rows, LANES), F32),
+            dma((4, lines)),
+            dma((4, lines)),
+            dma((2, 2)),
+            dma((2, 2)),
+            dma((3, 8)),
+            dma((3, 8)),
+            dma((3, 2)),
+            dma((lines, 2)),
+            dma((1,)),
+            dma((1,)),
+        ],
+        compiler_params=pltpu.CompilerParams(
+            collective_id=1, has_side_effects=True, vmem_limit_bytes=48 * 2**20
+        ),
+    )(ids, tensor, green)
+
+
 def solution(mesh):
     n = mesh.shape["ctr"]
     groups = mesh.shape["dist"]
@@ -271,6 +711,8 @@
         )
         vmem = pl.BlockSpec(memory_space=pltpu.VMEM)
         dma = pltpu.SemaphoreType.DMA
+        if n == 8 and groups % 2 == 0 and rows * 2 == BLK:
+            return on_line(n, groups, atoms, ids, tensor, green)
         return pl.pallas_call(
             functools.partial(kernel, n, groups, atoms),
             out_shape=jax.ShapeDtypeStruct((rows, n * rows), F32),

time: 72.7 us -> 71.7 us (0.986)
  the two profiles are of different devices: /device:TPU:0 before, /device:TPU:1 now
where the time goes in v1:
time: 71.7 us; the launch traced here: 71.4 us
  Pallas kernels  65.4 us (91%)
  local copies, waits for them, and re-layouts  5.81 us (8%)
    pallas_call x1, Pallas kernels, on_line(): pl.pallas_call(functools.partial(line_kernel, n, groups, atoms), out_shap...  65.4 us
    unnamed x16, local copies, waits for them, and re-layouts  5.22 us

profile of v1, /device:TPU:1, one launch (start us, length us, event | category | flops | bytes accessed | tf_op | source)
XLA Modules:
  0.0 71.4 jit_solution(16179065532970468227)
XLA Ops:
  0.0 0.0 copy-start.2
  0.0 0.8 %copy.13 = s32[16,4]{1,0:T(8,128)S(1)} copy(s32[16,4]{0,1:T(4,128)} %param.10) | data formatting | bytes 512 | tf_op args[3]
  0.8 0.1 reshape.18
  0.9 0.0 copy-done.2
  0.9 0.1 copy.10
  1.0 0.0 copy-start.3
  1.0 0.1 reshape.15
  1.1 0.6 copy-done.3
  1.7 0.1 copy.11
  1.8 0.0 copy-start.4
  1.8 0.1 reshape.16
  1.9 0.6 copy-done.4
  2.5 0.0 copy-start
  2.5 0.0 copy-start.1
  2.5 0.1 copy.12
  2.6 0.1 reshape.17
  2.7 0.5 copy-done
  3.2 0.0 copy-done.1
  3.3 0.2 reshape.19.green_ref
  3.5 1.8 %copy.16 = bf16[32,4,4096]{2,0,1:T(8,128)(2,1)S(1)} copy(bf16[32,4,4096]{2,1,0:T(4,128)(2,1)} %param.7) | data formatting | bytes 2097152 | tf_op args[0]
  5.3 65.4 %shard_map.73 = f32[32,256]{1,0:T(8,128)S(1)} custom-call(s32[832]{0:T(1024)S(1)} %pad_add_fusion.ids, bf16[4,32,4096]{2,1,0:T(8,128)(2,1)S(1)} %bitcast.3, bf16[8,64,64]{2,1,0:T(8,128)(2,1)S(1)} %reshape.19.green_ref), custom_call_target="tpu_custom_call" | custom-call | tf_op jit(solution)/shard_map/pallas_call | solution.py:654
  70.7 0.6 copy.18
  (2 shorter events, 0.0 us)
Async XLA Ops:
  0.0 0.9 %copy-start.2 = (s32[16,4,4]{0,2,1:T(4,128)S(1)}, s32[16,4,4]{0,2,1:T(4,128)}, u32[]{:S(2)}) copy-start(s32[16,4,4]{0,2,1:T(4,128)} %param.11) | copy-start | bytes 3076
  1.0 0.7 copy-start.3
  1.8 0.7 copy-start.4
  2.5 0.8 %copy-start = (bf16[4,4096]{1,0:T(4,128)(2,1)S(1)}, bf16[4,4096]{1,0:T(4,128)(2,1)}, u32[]{:S(2)}) copy-start(bf16[4,4096]{1,0:T(4,128)(2,1)} %param.8) | copy-start | bytes 98308
  2.5 0.8 %copy-start.1 = (bf16[4,4096]{1,0:T(4,128)(2,1)S(1)}, bf16[4,4096]{1,0:T(4,128)(2,1)}, u32[]{:S(2)}) copy-start(bf16[4,4096]{1,0:T(4,128)(2,1)} %param.9) | copy-start | bytes 98308

commit v2 on v1

--- a/solution.py
+++ b/solution.py
@@ -266,7 +266,7 @@
     return jnp.dot(a, b, preferred_element_type=F32)
 
 
-def line_kernel(n, groups, atoms, ids, t_ref, green_ref, out_ref, table, halves, moved, stack, swapped, tf, xg, wg, uf,
+def line_kernel(n, groups, atoms, ids, t_ref, green_ref, out_ref, table, halves, moved, stack, match_op, tf, xg, wg, uf,
                 first_op, second_op, gather, select, place, lift, turn_v, blk, cross, partner_in, cross_in,
                 g_send, g_recv, y_send, y_recv, m_send, m_recv, c_send, c_recv, p_send, p_recv):
     slots, rows, width = t_ref.shape
@@ -412,21 +412,21 @@
         third_hop.append(remote(at_home(c), across(c), g_send.at[2, k], g_recv.at[2, k], before, me))
         third_hop[-1].start()
     over_y(0, 1).start()
-
-    def relay(slot, k):
-        for a in {0: (1, 2), 1: (2,), 2: ()}[slot]:
-            @pl.when(place_at == a)
-            def _():
-                for x in range(pieces):
-                    over_z(slot, k, x, False, a).wait_recv()
-                    over_z(slot, k, x, False, a + 1).start()
-
-    relay(1, 0)
-    relay(0, 0)
+    for k in range(2):
+        over_y(1, k).start()
+
+    def relay(a, slot, k):
+        @pl.when(place_at == a)
+        def _():
+            for x in range(pieces):
+                over_z(slot, k, x, False, a).wait_recv()
+                over_z(slot, k, x, False, a + 1).start()
+
     from_y(0, 0).wait_recv()
     send_own(2)
-    relay(1, 1)
-    relay(0, 1)
+    relay(2, 1, 0)
+    relay(1, 0, 0)
+    relay(2, 1, 1)
 
     for k in range(lines):
         second_hop[k].wait_recv()
@@ -434,17 +434,11 @@
         third_hop.append(remote(at_home(c), across(c), g_send.at[3, k], g_recv.at[3, k], before, me))
         third_hop[-1].start()
 
-    from_y(0, 1).wait_recv()
-    send_own(3)
-    for k in range(2):
-        over_y(0, k).wait_send()
-        over_y(1, k).start()
+    relay(2, 1, 2)
+    relay(2, 0, 0)
+    relay(1, 0, 1)
     for copy in third_hop:
-        copy.wait()
-    for copy in first_hop + second_hop:
-        copy.wait_send()
-    relay(1, 2)
-    relay(0, 2)
+        copy.wait_recv()
 
     size = atoms * slots
     occ_at, virt_at, pair_at = size * slots, 2 * size * slots, 3 * size * slots
@@ -482,6 +476,10 @@
     size_op = slots * BLK
     unit = (iota((size_op, size_op), 0) == iota((size_op, size_op), 1)).astype(BF16)
     first_op[0] = nt(unit, nn(gather[...], place[...]).astype(BF16)).astype(BF16)
+
+    from_y(0, 1).wait_recv()
+    send_own(3)
+    relay(2, 0, 1)
 
     def operators(slot, a):
         other = atom_at(a)
@@ -515,6 +513,16 @@
         def _():
             operators(slot, used[slot][0])
 
+    r_, c_ = iota((LANES, LANES), 0), iota((LANES, LANES), 1)
+    for slot in used:
+        other = atom_at(used[slot][0])
+        match = jnp.zeros((LANES, LANES), F32)
+        for s in range(slots):
+            for t in range(slots):
+                hit = jnp.where(ids[pair_at + atom * slots + s] == ids[pair_at + other * slots + t], 1.0, 0.0)
+                match = jnp.where((r_ // half == s) & (c_ // half == t), hit.astype(F32), match)
+        match_op[:, slot * LANES:(slot + 1) * LANES] = jnp.where(r_ % half == c_ % half, match, 0.0).astype(BF16)
+
     lanes2 = (iota((BLK, 2 * LANES), 1) // half) % slots
 
     def one_stack(k, at_rows):
@@ -532,6 +540,16 @@
         for m in range(BLK):
             stack[k, at_rows, m * LANES:(m + 1) * LANES] = uf[pl.ds(m, part_rows, stride=BLK), :].astype(BF16)
 
+    def reorder(at_rows):
+        x = jnp.concatenate([stack[0, at_rows, m * LANES:(m + 1) * LANES] for m in range(BLK)], axis=0)
+        got = nn(x, match_op[...]).astype(BF16)
+        below = pl.ds(at_rows.start + BLK, part_rows)
+        for m in range(BLK):
+            for slot in used:
+                stack[1 + slot, below, m * LANES:(m + 1) * LANES] = got[
+                    m * part_rows:(m + 1) * part_rows, slot * LANES:(slot + 1) * LANES
+                ]
+
     def transform(g):
         at_rows = rows_of(g)
         for h in range(2):
@@ -552,13 +570,21 @@
 
         lax.fori_loop(0, 1 + len(used), each, 0)
 
-    for g in range(4):
-        if g >= 2:
-            from_y(1, g - 2).wait_recv()
-        transform(g)
-        if g == 0:
-            relay(1, 3)
-            relay(0, 3)
+        @pl.when(place_at > 0)
+        def _():
+            reorder(at_rows)
+
+    relay(1, 0, 2)
+    relay(2, 1, 3)
+    transform(0)
+    relay(2, 0, 2)
+    relay(1, 0, 3)
+    transform(1)
+    from_y(1, 0).wait_recv()
+    transform(2)
+    relay(2, 0, 3)
+    from_y(1, 1).wait_recv()
+    transform(3)
 
     for c in range(lines):
         blk[c] = jnp.zeros((BLK, LANES), F32)
@@ -566,7 +592,7 @@
     def lay(x):
         return jnp.concatenate([x, jnp.zeros((BLK, LANES - BLK), F32)], axis=1)
 
-    blk[high] = lay(nt(stack[0], halves[low]))
+    blk[high] = lay(nt(stack[0, :BLK], halves[low]))
 
     def returned(slot, y):
         a = used[slot][0]
@@ -586,25 +612,13 @@
                 def _():
                     for x in range(pieces):
                         over_z(slot, k, x, False, a).wait_recv()
-        cross[slot] = lay(nt(moved[slot], stack[1 + slot]))
+        both = nt(moved[slot], stack[1 + slot])
+        cross[slot] = both
         for y in range(2):
             returned(slot, y).start()
-        other = atom_at(a)
-        r_, c_ = iota((LANES, LANES), 0), iota((LANES, LANES), 1)
-        match = jnp.zeros((LANES, LANES), F32)
-        for s in range(slots):
-            for t in range(slots):
-                hit = jnp.where(ids[pair_at + atom * slots + s] == ids[pair_at + other * slots + t], 1.0, 0.0)
-                match = jnp.where((r_ // half == s) & (c_ // half == t), hit.astype(F32), match)
-        match = jnp.where(r_ % half == c_ % half, match, 0.0).astype(BF16)
-        for m in range(0, BLK, 8):
-            x = jnp.concatenate([stack[0, :, (m + p) * LANES:(m + p + 1) * LANES] for p in range(8)], axis=0)
-            got = nn(x, match).astype(BF16)
-            for p in range(8):
-                swapped[:, (m + p) * LANES:(m + p + 1) * LANES] = got[p * BLK:(p + 1) * BLK]
-        blk[flip(a)] = lay(nt(swapped[...], moved[slot]))
-
-    for slot in (1, 0, 2):
+        blk[flip(a)] = lay(both.T[BLK:])
+
+    for slot in (2, 1, 0):
         @pl.when(wanted_here(slot))
         def _():
             product(slot)
@@ -627,7 +641,10 @@
     tiles = [(blk[c, own_rows] + partner_in[c])[:, :BLK] for c in range(lines)]
     out_ref[...] = jnp.concatenate(tiles, axis=1)
 
+    for copy in first_hop + second_hop + third_hop:
+        copy.wait_send()
     for k in range(2):
+        over_y(0, k).wait_send()
         over_y(1, k).wait_send()
     for slot, senders in {0: (0, 1, 2), 1: (1, 2), 2: (3,)}.items():
         for a in senders:
@@ -660,8 +677,8 @@
             pltpu.VMEM((2 * n * blocks, BLK, LANES), BF16),
             pltpu.VMEM((2, BLK, deep), BF16),
             pltpu.VMEM((3, BLK, deep), BF16),
-            pltpu.VMEM((4, BLK, deep), BF16),
-            pltpu.VMEM((BLK, deep), BF16),
+            pltpu.VMEM((4, 2 * BLK, deep), BF16),
+            pltpu.VMEM((LANES, 3 * LANES), BF16),
             pltpu.VMEM((2, part_rows * BLK, LANES), F32),
             pltpu.VMEM((part_rows * BLK, 2 * LANES), BF16),
             pltpu.VMEM((part_rows, slots * BLK, LANES), BF16),

time: 71.7 us -> 64.1 us (0.89)
  the two profiles are of different devices: /device:TPU:1 before, /device:TPU:0 now
where the time goes in v2:
time: 64.1 us; the launch traced here: 63.8 us
  Pallas kernels  57.9 us (90%)
  local copies, waits for them, and re-layouts  5.81 us (9%)
    pallas_call x1, Pallas kernels, on_line(): pl.pallas_call(functools.partial(line_kernel, n, groups, atoms), out_shap...  57.9 us
    unnamed x16, local copies, waits for them, and re-layouts  5.22 us

profile of v2, /device:TPU:0, one launch (start us, length us, event | category | flops | bytes accessed | tf_op | source)
XLA Modules:
  0.0 63.8 jit_solution(12222059041109355615)
XLA Ops:
  0.0 0.0 copy-start.2
  0.0 0.8 %copy.13 = s32[16,4]{1,0:T(8,128)S(1)} copy(s32[16,4]{0,1:T(4,128)} %param.10) | data formatting | bytes 512 | tf_op args[3]
  0.8 0.1 reshape.18
  0.9 0.0 copy-done.2
  0.9 0.1 copy.10
  1.0 0.0 copy-start.3
  1.0 0.1 reshape.15
  1.1 0.6 copy-done.3
  1.7 0.1 copy.11
  1.8 0.0 copy-start.4
  1.8 0.1 reshape.16
  1.9 0.6 copy-done.4
  2.5 0.0 copy-start
  2.5 0.0 copy-start.1
  2.5 0.1 copy.12
  2.6 0.1 reshape.17
  2.7 0.5 copy-done
  3.2 0.0 copy-done.1
  3.3 0.2 reshape.19.green_ref
  3.5 1.8 %copy.16 = bf16[32,4,4096]{2,0,1:T(8,128)(2,1)S(1)} copy(bf16[32,4,4096]{2,1,0:T(4,128)(2,1)} %param.7) | data formatting | bytes 2097152 | tf_op args[0]
  5.3 57.9 %shard_map.73 = f32[32,256]{1,0:T(8,128)S(1)} custom-call(s32[832]{0:T(1024)S(1)} %pad_add_fusion.ids, bf16[4,32,4096]{2,1,0:T(8,128)(2,1)S(1)} %bitcast.3, bf16[8,64,64]{2,1,0:T(8,128)(2,1)S(1)} %reshape.19.green_ref), custom_call_target="tpu_custom_call" | custom-call | tf_op jit(solution)/shard_map/pallas_call | solution.py:671
  63.2 0.6 copy.18
  (2 shorter events, 0.0 us)
Async XLA Ops:
  0.0 0.9 %copy-start.2 = (s32[16,4,4]{0,2,1:T(4,128)S(1)}, s32[16,4,4]{0,2,1:T(4,128)}, u32[]{:S(2)}) copy-start(s32[16,4,4]{0,2,1:T(4,128)} %param.11) | copy-start | bytes 3076
  1.0 0.7 %copy-start.3 = (s32[16,4,4]{0,2,1:T(4,128)S(1)}, s32[16,4,4]{0,2,1:T(4,128)}, u32[]{:S(2)}) copy-start(s32[16,4,4]{0,2,1:T(4,128)} %param.12) | copy-start | bytes 3076
  1.8 0.7 %copy-start.4 = (s32[16,4,4]{0,2,1:T(4,128)S(1)}, s32[16,4,4]{0,2,1:T(4,128)}, u32[]{:S(2)}) copy-start(s32[16,4,4]{0,2,1:T(4,128)} %param.13) | copy-start | bytes 3076
  2.5 0.8 %copy-start = (bf16[4,4096]{1,0:T(4,128)(2,1)S(1)}, bf16[4,4096]{1,0:T(4,128)(2,1)}, u32[]{:S(2)}) copy-start(bf16[4,4096]{1,0:T(4,128)(2,1)} %param.8) | copy-start | bytes 98308
  2.5 0.8 %copy-start.1 = (bf16[4,4096]{1,0:T(4,128)(2,1)S(1)}, bf16[4,4096]{1,0:T(4,128)(2,1)}, u32[]{:S(2)}) copy-start(bf16[4,4096]{1,0:T(4,128)(2,1)} %param.9) | copy-start | bytes 98308

commit v3 on v2

--- a/solution.py
+++ b/solution.py
@@ -479,7 +479,6 @@
 
     from_y(0, 1).wait_recv()
     send_own(3)
-    relay(2, 0, 1)
 
     def operators(slot, a):
         other = atom_at(a)
@@ -525,20 +524,32 @@
 
     lanes2 = (iota((BLK, 2 * LANES), 1) // half) % slots
 
-    def one_stack(k, at_rows):
+    def first(k, u):
         got = nn(xg[...], second_op[k]).astype(BF16)
         for i in range(part_rows):
             for t in range(slots):
-                wg[i, t * BLK:(t + 1) * BLK, :] = got[i * BLK:(i + 1) * BLK, t * LANES:(t + 1) * LANES]
+                wg[u, i, t * BLK:(t + 1) * BLK, :] = got[i * BLK:(i + 1) * BLK, t * LANES:(t + 1) * LANES]
+
+    def second(k, u):
         for p in range(part_rows // 2):
-            both = nn(first_op[k], jnp.concatenate([wg[2 * p], wg[2 * p + 1]], axis=1))
+            both = nn(first_op[k], jnp.concatenate([wg[u, 2 * p], wg[u, 2 * p + 1]], axis=1))
             res = both[:BLK]
             for o in range(1, slots):
                 res = jnp.where(lanes2 == o, both[o * BLK:(o + 1) * BLK], res)
             for x in range(2):
-                uf[(2 * p + x) * BLK:(2 * p + x + 1) * BLK, :] = res[:, x * LANES:(x + 1) * LANES]
+                uf[u, (2 * p + x) * BLK:(2 * p + x + 1) * BLK, :] = res[:, x * LANES:(x + 1) * LANES]
+
+    def keep(k, u, at_rows):
         for m in range(BLK):
-            stack[k, at_rows, m * LANES:(m + 1) * LANES] = uf[pl.ds(m, part_rows, stride=BLK), :].astype(BF16)
+            stack[k, at_rows, m * LANES:(m + 1) * LANES] = uf[u, pl.ds(m, part_rows, stride=BLK), :].astype(BF16)
+
+    def two_stacks(k, at_rows):
+        for u in range(2):
+            first(k + u, u)
+        for u in range(2):
+            second(k + u, u)
+        for u in range(2):
+            keep(k + u, u, at_rows)
 
     def reorder(at_rows):
         x = jnp.concatenate([stack[0, at_rows, m * LANES:(m + 1) * LANES] for m in range(BLK)], axis=0)
@@ -550,8 +561,7 @@
                     m * part_rows:(m + 1) * part_rows, slot * LANES:(slot + 1) * LANES
                 ]
 
-    def transform(g):
-        at_rows = rows_of(g)
+    def spread(at_rows):
         for h in range(2):
             for m in range(BLK):
                 tf[h, m * part_rows:(m + 1) * part_rows, :] = halves[h, at_rows, m * LANES:(m + 1) * LANES].astype(F32)
@@ -560,31 +570,35 @@
                     h, pl.ds(i, BLK, stride=part_rows), :
                 ].astype(BF16)
 
-        def each(k, carry):
-            hit = (k == 0) | ((k == 1) & wanted_here(0)) | ((k == 2) & wanted_here(1)) | ((k == 3) & wanted_here(2))
-
-            @pl.when(hit)
+    due = ((0, 2, 0, 1), (1, 2, 1, 3), (1, 1, 0, 2), (2, 2, 0, 2), (4, 1, 0, 3), (5, 2, 0, 3))
+
+    def step(g, carry):
+        y = jnp.where(g < 2, low, 1 - low)
+        at_rows = pl.ds(pl.multiple_of(y * rows + lax.rem(g, 2) * part_rows, part_rows), part_rows)
+        for x in range(2):
+            @pl.when(g == 2 + x)
             def _():
-                one_stack(k, at_rows)
-            return carry
-
-        lax.fori_loop(0, 1 + len(used), each, 0)
-
-        @pl.when(place_at > 0)
+                from_y(1, x).wait_recv()
+
+        def relays(side):
+            for at, a, slot, group in due:
+                if at % 2 == side:
+                    @pl.when(g == at // 2)
+                    def _():
+                        relay(a, slot, group)
+
+        spread(at_rows)
+        two_stacks(0, at_rows)
+        reorder(at_rows)
+        relays(0)
+
+        @pl.when(place_at >= 2)
         def _():
-            reorder(at_rows)
-
-    relay(1, 0, 2)
-    relay(2, 1, 3)
-    transform(0)
-    relay(2, 0, 2)
-    relay(1, 0, 3)
-    transform(1)
-    from_y(1, 0).wait_recv()
-    transform(2)
-    relay(2, 0, 3)
-    from_y(1, 1).wait_recv()
-    transform(3)
+            two_stacks(2, at_rows)
+        relays(1)
+        return carry
+
+    lax.fori_loop(0, 4, step, 0)
 
     for c in range(lines):
         blk[c] = jnp.zeros((BLK, LANES), F32)
@@ -681,8 +695,8 @@
             pltpu.VMEM((LANES, 3 * LANES), BF16),
             pltpu.VMEM((2, part_rows * BLK, LANES), F32),
             pltpu.VMEM((part_rows * BLK, 2 * LANES), BF16),
-            pltpu.VMEM((part_rows, slots * BLK, LANES), BF16),
-            pltpu.VMEM((part_rows * BLK, LANES), F32),
+            pltpu.VMEM((2, part_rows, slots * BLK, LANES), BF16),
+            pltpu.VMEM((2, part_rows * BLK, LANES), F32),
             pltpu.VMEM((4, slots * BLK, slots * BLK), BF16),
             pltpu.VMEM((4, 2 * LANES, slots * LANES), BF16),
             pltpu.VMEM((slots * BLK, slots * LANES), BF16),

time: 64.1 us -> 58.3 us (0.910)
  Pallas kernels: 57.9 us -> 52 us
    pallas_call x1, Pallas kernels: 57.9 us -> 52 us  [on_line(): pl.pallas_call(functools.partial(line_kernel, n, groups, atoms), out_shap...]
where the time goes in v3:
time: 58.3 us; the launch traced here: 57.9 us
  Pallas kernels  52 us (89%)
  local copies, waits for them, and re-layouts  5.81 us (10%)
    pallas_call x1, Pallas kernels, on_line(): pl.pallas_call(functools.partial(line_kernel, n, groups, atoms), out_shap...  52 us
    unnamed x16, local copies, waits for them, and re-layouts  5.22 us

profile of v3, /device:TPU:0, one launch (start us, length us, event | category | flops | bytes accessed | tf_op | source)
XLA Modules:
  0.0 57.9 jit_solution(14948420087896665071)
XLA Ops:
  0.0 0.0 copy-start.2
  0.0 0.8 %copy.13 = s32[16,4]{1,0:T(8,128)S(1)} copy(s32[16,4]{0,1:T(4,128)} %param.10) | data formatting | bytes 512 | tf_op args[3]
  0.8 0.1 reshape.18
  0.9 0.0 copy-done.2
  0.9 0.1 copy.10
  1.0 0.0 copy-start.3
  1.0 0.1 reshape.15
  1.1 0.6 %copy-done.3 = s32[16,4,4]{0,2,1:T(4,128)S(1)} copy-done((s32[16,4,4]{0,2,1:T(4,128)S(1)}, s32[16,4,4]{0,2,1:T(4,128)}, u32[]{:S(2)}) %copy-start.3) | copy-done | bytes 1048
  1.7 0.1 copy.11
  1.8 0.0 copy-start.4
  1.8 0.1 reshape.16
  1.9 0.6 %copy-done.4 = s32[16,4,4]{0,2,1:T(4,128)S(1)} copy-done((s32[16,4,4]{0,2,1:T(4,128)S(1)}, s32[16,4,4]{0,2,1:T(4,128)}, u32[]{:S(2)}) %copy-start.4) | copy-done | bytes 1048
  2.5 0.0 copy-start
  2.5 0.0 copy-start.1
  2.5 0.1 copy.12
  2.6 0.1 reshape.17
  2.7 0.5 copy-done
  3.2 0.0 copy-done.1
  3.3 0.2 reshape.19.green_ref
  3.5 1.8 %copy.16 = bf16[32,4,4096]{2,0,1:T(8,128)(2,1)S(1)} copy(bf16[32,4,4096]{2,1,0:T(4,128)(2,1)} %param.7) | data formatting | bytes 2097152 | tf_op args[0]
  5.3 52.0 %shard_map.73 = f32[32,256]{1,0:T(8,128)S(1)} custom-call(s32[832]{0:T(1024)S(1)} %pad_add_fusion.ids, bf16[4,32,4096]{2,1,0:T(8,128)(2,1)S(1)} %bitcast.3, bf16[8,64,64]{2,1,0:T(8,128)(2,1)S(1)} %reshape.19.green_ref), custom_call_target="tpu_custom_call" | custom-call | tf_op jit(solution)/shard_map/pallas_call | solution.py:685
  57.3 0.6 %copy.18 = f32[32,256]{1,0:T(8,128)} copy(f32[32,256]{1,0:T(8,128)S(1)} %shard_map.73) | data formatting | bytes 65536
  (2 shorter events, 0.0 us)
Async XLA Ops:
  0.0 0.9 %copy-start.2 = (s32[16,4,4]{0,2,1:T(4,128)S(1)}, s32[16,4,4]{0,2,1:T(4,128)}, u32[]{:S(2)}) copy-start(s32[16,4,4]{0,2,1:T(4,128)} %param.11) | copy-start | bytes 3076
  1.0 0.7 %copy-start.3 = (s32[16,4,4]{0,2,1:T(4,128)S(1)}, s32[16,4,4]{0,2,1:T(4,128)}, u32[]{:S(2)}) copy-start(s32[16,4,4]{0,2,1:T(4,128)} %param.12) | copy-start | bytes 3076
  1.8 0.7 %copy-start.4 = (s32[16,4,4]{0,2,1:T(4,128)S(1)}, s32[16,4,4]{0,2,1:T(4,128)}, u32[]{:S(2)}) copy-start(s32[16,4,4]{0,2,1:T(4,128)} %param.13) | copy-start | bytes 3076
  2.5 0.8 %copy-start = (bf16[4,4096]{1,0:T(4,128)(2,1)S(1)}, bf16[4,4096]{1,0:T(4,128)(2,1)}, u32[]{:S(2)}) copy-start(bf16[4,4096]{1,0:T(4,128)(2,1)} %param.8) | copy-start | bytes 98308
  2.5 0.8 %copy-start.1 = (bf16[4,4096]{1,0:T(4,128)(2,1)S(1)}, bf16[4,4096]{1,0:T(4,128)(2,1)}, u32[]{:S(2)}) copy-start(bf16[4,4096]{1,0:T(4,128)(2,1)} %param.9) | copy-start | bytes 98308

commit v4 on v3

--- a/solution.py
+++ b/solution.py
@@ -266,7 +266,7 @@
     return jnp.dot(a, b, preferred_element_type=F32)
 
 
-def line_kernel(n, groups, atoms, ids, t_ref, green_ref, out_ref, table, halves, moved, stack, match_op, tf, xg, wg, uf,
+def line_kernel(n, groups, atoms, source_ids, occ_ids, virt_ids, pair_ids, t_ref, green_ref, out_ref, table, halves, moved, stack, match_op, tf, xg, wg, uf,
                 first_op, second_op, gather, select, place, lift, turn_v, blk, cross, partner_in, cross_in,
                 g_send, g_recv, y_send, y_recv, m_send, m_recv, c_send, c_recv, p_send, p_recv):
     slots, rows, width = t_ref.shape
@@ -365,22 +365,34 @@
     ]
     for copy in first_hop:
         copy.start()
+    second_hop, third_hop = [], []
+
+    def onward(k):
+        c = line(lines - k) + low
+        second_hop.append(remote(at_home(c), at_home(c), g_send.at[1, k], g_recv.at[1, k], dist, partner))
+        second_hop[-1].start()
+        third_hop.append(remote(at_home(c), across(c), g_send.at[2, k], g_recv.at[2, k], before, me))
+        third_hop[-1].start()
+
+    onward(0)
 
     def rows_of(k):
         y = low if k < 2 else 1 - low
         return pl.ds(pl.multiple_of(y * rows + (k % 2) * part_rows, part_rows), part_rows)
 
-    def over_y(phase, k):
-        h = 1 - low if phase == 0 else low
-        at = halves.at[h, rows_of(k)]
-        return remote(at, at, y_send.at[phase, k], y_recv.at[phase, k], dist, partner)
-
-    def from_y(phase, k):
-        at = halves.at[low if phase == 0 else 1 - low, rows_of(2 + k)]
-        return remote(at, at, y_send.at[phase, k], y_recv.at[phase, k], dist, partner)
-
     pieces = 2
     piece = deep // pieces
+
+    def over_y(phase, k, x):
+        h = 1 - low if phase == 0 else low
+        at = halves.at[h, rows_of(k), pl.ds(x * piece, piece)]
+        sem = k * pieces + x
+        return remote(at, at, y_send.at[phase, sem], y_recv.at[phase, sem], dist, partner)
+
+    def from_y(phase, k, x):
+        at = halves.at[low if phase == 0 else 1 - low, rows_of(2 + k), pl.ds(x * piece, piece)]
+        sem = k * pieces + x
+        return remote(at, at, y_send.at[phase, sem], y_recv.at[phase, sem], dist, partner)
 
     def over_z(slot, k, x, own, to):
         at, lanes = rows_of(k), pl.ds(x * piece, piece)
@@ -390,30 +402,37 @@
             src, moved.at[slot, at, lanes], m_send.at[slot, sem], m_recv.at[slot, sem], dist, at_place(to, low)
         )
 
+    def spread(g):
+        at_rows = rows_of(g)
+        for h in range(2):
+            for m in range(BLK):
+                tf[h, m * part_rows:(m + 1) * part_rows, :] = halves[h, at_rows, m * LANES:(m + 1) * LANES].astype(F32)
+            for i in range(part_rows):
+                xg[g % 2, i * BLK:(i + 1) * BLK, h * LANES:(h + 1) * LANES] = tf[
+                    h, pl.ds(i, BLK, stride=part_rows), :
+                ].astype(BF16)
+
     starts = {0: (0, 1), 1: (1, 2), 3: (2, 2)}
 
-    def send_own(k):
-        for a, (slot, to) in starts.items():
+    def send_own(k, places):
+        for a in places:
+            slot, to = starts[a]
+
             @pl.when(place_at == a)
             def _():
                 for x in range(pieces):
                     over_z(slot, k, x, True, to).start()
 
-    over_y(0, 0).start()
+    over_y(0, 0, 0).start()
+    over_y(0, 0, 1).start()
     for k in range(2):
-        send_own(k)
-    second_hop, third_hop = [], []
-    for k in range(lines):
-        if k:
-            first_hop[k - 1].wait_recv()
-        c = line(lines - k) + low
-        second_hop.append(remote(at_home(c), at_home(c), g_send.at[1, k], g_recv.at[1, k], dist, partner))
-        second_hop[-1].start()
-        third_hop.append(remote(at_home(c), across(c), g_send.at[2, k], g_recv.at[2, k], before, me))
-        third_hop[-1].start()
-    over_y(0, 1).start()
-    for k in range(2):
-        over_y(1, k).start()
+        send_own(k, (0, 1))
+    for k in range(1, lines):
+        first_hop[k - 1].wait_recv()
+        onward(k)
+    for phase, k in ((0, 1), (1, 0), (1, 1)):
+        for x in range(pieces):
+            over_y(phase, k, x).start()
 
     def relay(a, slot, k):
         @pl.when(place_at == a)
@@ -422,26 +441,31 @@
                 over_z(slot, k, x, False, a).wait_recv()
                 over_z(slot, k, x, False, a + 1).start()
 
-    from_y(0, 0).wait_recv()
-    send_own(2)
-    relay(2, 1, 0)
-    relay(1, 0, 0)
-    relay(2, 1, 1)
-
-    for k in range(lines):
+    def third(k):
         second_hop[k].wait_recv()
         c = line(lines - k) + 1 - low
         third_hop.append(remote(at_home(c), across(c), g_send.at[3, k], g_recv.at[3, k], before, me))
         third_hop[-1].start()
 
+    third(0)
+    for x in range(pieces):
+        from_y(0, 0, x).wait_recv()
+    send_own(2, (0, 1))
+    for k in range(1, lines):
+        third(k)
+    relay(1, 0, 0)
+    relay(2, 1, 0)
+    relay(2, 1, 1)
+    relay(1, 0, 1)
+    spread(0)
+    spread(1)
     relay(2, 1, 2)
     relay(2, 0, 0)
-    relay(1, 0, 1)
     for copy in third_hop:
         copy.wait_recv()
-
-    size = atoms * slots
-    occ_at, virt_at, pair_at = size * slots, 2 * size * slots, 3 * size * slots
+    for k in range(3):
+        send_own(k, (3,))
+
     total = n * blocks * groups
     base = dist * n * blocks
     atom = dist * lines + high
@@ -456,13 +480,12 @@
     def feeding(a, s, j):
         r, live = jnp.int32(0), jnp.int32(0)
         for x in range(slots):
-            hit = ids[(a * slots + s) * slots + x] == j
+            hit = source_ids[s, x, a] == j
             r, live = jnp.where(hit, x, r), jnp.where(hit, 1, live)
         return r, live
 
     def green(a, s, r, live):
-        at = (a * slots + s) * slots + r
-        return position(ids[occ_at + at]), position(ids[virt_at + at]), live.astype(F32)
+        return position(occ_ids[s, r, a]), position(virt_ids[s, r, a]), live.astype(F32)
 
     for t in range(slots):
         virt = []
@@ -470,23 +493,24 @@
             r, live = feeding(atom, o, t)
             occ_pos, virt_pos, live = green(atom, o, r, live)
             virt.append((table[virt_pos].astype(F32) * live).astype(BF16))
-            gather[t * BLK:(t + 1) * BLK, o * LANES:(o + 1) * LANES] = table[occ_pos]
+            gather[3, t * BLK:(t + 1) * BLK, o * LANES:(o + 1) * LANES] = table[occ_pos]
         b = nt(turn_v[...], jnp.concatenate(virt, axis=1)).astype(BF16)
         second_op[0, :, t * LANES:(t + 1) * LANES] = nt(lift[t][:, :BLK], b).astype(BF16)
     size_op = slots * BLK
     unit = (iota((size_op, size_op), 0) == iota((size_op, size_op), 1)).astype(BF16)
-    first_op[0] = nt(unit, nn(gather[...], place[...]).astype(BF16)).astype(BF16)
-
-    from_y(0, 1).wait_recv()
-    send_own(3)
+    first_op[0] = nt(unit, nn(gather[3], place[...]).astype(BF16)).astype(BF16)
+
+    for x in range(pieces):
+        from_y(0, 1, x).wait_recv()
+    send_own(3, (0, 1, 3))
 
     def operators(slot, a):
         other = atom_at(a)
         for t in range(slots):
-            pair = ids[pair_at + atom * slots + t]
+            pair = pair_ids[t, atom]
             s, met = jnp.int32(0), jnp.int32(0)
             for x in range(slots):
-                hit = ids[pair_at + other * slots + x] == pair
+                hit = pair_ids[x, other] == pair
                 s, met = jnp.where(hit, x, s), jnp.where(hit, 1, met)
             virt = []
             for o in range(slots):
@@ -495,9 +519,9 @@
                 virt.append(
                     (table[virt_pos, pl.ds(pl.multiple_of(low * half, half), half), :].astype(F32) * live).astype(BF16)
                 )
-                gather[o * BLK:(o + 1) * BLK, t * LANES:(t + 1) * LANES] = table[occ_pos]
+                gather[slot, o * BLK:(o + 1) * BLK, t * LANES:(t + 1) * LANES] = table[occ_pos]
             second_op[1 + slot, :, t * LANES:(t + 1) * LANES] = nt(lift[t], jnp.concatenate(virt, axis=0)).astype(BF16)
-        first_op[1 + slot] = nn(gather[...], place[...]).astype(BF16)
+        first_op[1 + slot] = nn(gather[slot], place[...]).astype(BF16)
 
     used = {0: (0, (1, 2, 3)), 1: (1, (2, 3)), 2: (3, (2,))}
 
@@ -508,9 +532,7 @@
         return hit
 
     for slot in used:
-        @pl.when(wanted_here(slot))
-        def _():
-            operators(slot, used[slot][0])
+        operators(slot, used[slot][0])
 
     r_, c_ = iota((LANES, LANES), 0), iota((LANES, LANES), 1)
     for slot in used:
@@ -518,14 +540,14 @@
         match = jnp.zeros((LANES, LANES), F32)
         for s in range(slots):
             for t in range(slots):
-                hit = jnp.where(ids[pair_at + atom * slots + s] == ids[pair_at + other * slots + t], 1.0, 0.0)
+                hit = jnp.where(pair_ids[s, atom] == pair_ids[t, other], 1.0, 0.0)
                 match = jnp.where((r_ // half == s) & (c_ // half == t), hit.astype(F32), match)
         match_op[:, slot * LANES:(slot + 1) * LANES] = jnp.where(r_ % half == c_ % half, match, 0.0).astype(BF16)
 
     lanes2 = (iota((BLK, 2 * LANES), 1) // half) % slots
 
-    def first(k, u):
-        got = nn(xg[...], second_op[k]).astype(BF16)
+    def first(k, u, g):
+        got = nn(xg[lax.rem(g, 2)], second_op[k]).astype(BF16)
         for i in range(part_rows):
             for t in range(slots):
                 wg[u, i, t * BLK:(t + 1) * BLK, :] = got[i * BLK:(i + 1) * BLK, t * LANES:(t + 1) * LANES]
@@ -543,9 +565,9 @@
         for m in range(BLK):
             stack[k, at_rows, m * LANES:(m + 1) * LANES] = uf[u, pl.ds(m, part_rows, stride=BLK), :].astype(BF16)
 
-    def two_stacks(k, at_rows):
+    def two_stacks(k, at_rows, g):
         for u in range(2):
-            first(k + u, u)
+            first(k + u, u, g)
         for u in range(2):
             second(k + u, u)
         for u in range(2):
@@ -561,16 +583,7 @@
                     m * part_rows:(m + 1) * part_rows, slot * LANES:(slot + 1) * LANES
                 ]
 
-    def spread(at_rows):
-        for h in range(2):
-            for m in range(BLK):
-                tf[h, m * part_rows:(m + 1) * part_rows, :] = halves[h, at_rows, m * LANES:(m + 1) * LANES].astype(F32)
-            for i in range(part_rows):
-                xg[i * BLK:(i + 1) * BLK, h * LANES:(h + 1) * LANES] = tf[
-                    h, pl.ds(i, BLK, stride=part_rows), :
-                ].astype(BF16)
-
-    due = ((0, 2, 0, 1), (1, 2, 1, 3), (1, 1, 0, 2), (2, 2, 0, 2), (4, 1, 0, 3), (5, 2, 0, 3))
+    due = ((0, 2, 0, 1), (1, 2, 1, 3), (0, 1, 0, 2), (2, 2, 0, 2), (2, 1, 0, 3), (4, 2, 0, 3))
 
     def step(g, carry):
         y = jnp.where(g < 2, low, 1 - low)
@@ -578,7 +591,9 @@
         for x in range(2):
             @pl.when(g == 2 + x)
             def _():
-                from_y(1, x).wait_recv()
+                for p in range(pieces):
+                    from_y(1, x, p).wait_recv()
+                spread(2 + x)
 
         def relays(side):
             for at, a, slot, group in due:
@@ -587,14 +602,13 @@
                     def _():
                         relay(a, slot, group)
 
-        spread(at_rows)
-        two_stacks(0, at_rows)
+        two_stacks(0, at_rows, g)
         reorder(at_rows)
         relays(0)
 
         @pl.when(place_at >= 2)
         def _():
-            two_stacks(2, at_rows)
+            two_stacks(2, at_rows, g)
         relays(1)
         return carry
 
@@ -606,7 +620,6 @@
     def lay(x):
         return jnp.concatenate([x, jnp.zeros((BLK, LANES - BLK), F32)], axis=1)
 
-    blk[high] = lay(nt(stack[0, :BLK], halves[low]))
 
     def returned(slot, y):
         a = used[slot][0]
@@ -626,17 +639,19 @@
                 def _():
                     for x in range(pieces):
                         over_z(slot, k, x, False, a).wait_recv()
-        both = nt(moved[slot], stack[1 + slot])
-        cross[slot] = both
+        both = nt(stack[1 + slot], moved[slot])
+        both = jnp.concatenate([both, jnp.zeros((2 * BLK, LANES - BLK), F32)], axis=1)
+        cross[slot] = both.T[:BLK]
         for y in range(2):
             returned(slot, y).start()
-        blk[flip(a)] = lay(both.T[BLK:])
+        blk[flip(a)] = both[BLK:]
 
     for slot in (2, 1, 0):
         @pl.when(wanted_here(slot))
         def _():
             product(slot)
 
+    blk[high] = lay(nt(stack[0, :BLK], halves[low]))
     other_rows = pl.ds(pl.multiple_of((1 - low) * rows, rows), rows)
     to_partner = remote(blk.at[:, other_rows], partner_in, p_send.at[0], p_recv.at[0], dist, partner)
     to_partner.start()
@@ -658,8 +673,9 @@
     for copy in first_hop + second_hop + third_hop:
         copy.wait_send()
     for k in range(2):
-        over_y(0, k).wait_send()
-        over_y(1, k).wait_send()
+        for x in range(pieces):
+            over_y(0, k, x).wait_send()
+            over_y(1, k, x).wait_send()
     for slot, senders in {0: (0, 1, 2), 1: (1, 2), 2: (3,)}.items():
         for a in senders:
             @pl.when(place_at == a)
@@ -674,7 +690,7 @@
                 returned(slot, y).wait_send()
 
 
-def on_line(n, groups, atoms, ids, tensor, green):
+def on_line(n, groups, atoms, source, occ, virt, pairs, tensor, green):
     slots, rows, width = tensor.shape
     blocks = green.shape[0] // 2
     lines = n // 2
@@ -685,7 +701,7 @@
     return pl.pallas_call(
         functools.partial(line_kernel, n, groups, atoms),
         out_shape=jax.ShapeDtypeStruct((rows, lines * BLK), F32),
-        in_specs=[pl.BlockSpec(memory_space=pltpu.SMEM), vmem, vmem],
+        in_specs=[pl.BlockSpec(memory_space=pltpu.SMEM)] * 4 + [vmem, vmem],
         out_specs=vmem,
         scratch_shapes=[
             pltpu.VMEM((2 * n * blocks, BLK, LANES), BF16),
@@ -694,12 +710,12 @@
             pltpu.VMEM((4, 2 * BLK, deep), BF16),
             pltpu.VMEM((LANES, 3 * LANES), BF16),
             pltpu.VMEM((2, part_rows * BLK, LANES), F32),
-            pltpu.VMEM((part_rows * BLK, 2 * LANES), BF16),
+            pltpu.VMEM((2, part_rows * BLK, 2 * LANES), BF16),
             pltpu.VMEM((2, part_rows, slots * BLK, LANES), BF16),
             pltpu.VMEM((2, part_rows * BLK, LANES), F32),
             pltpu.VMEM((4, slots * BLK, slots * BLK), BF16),
             pltpu.VMEM((4, 2 * LANES, slots * LANES), BF16),
-            pltpu.VMEM((slots * BLK, slots * LANES), BF16),
+            pltpu.VMEM((4, slots * BLK, slots * LANES), BF16),
             pltpu.VMEM((slots * LANES, slots * LANES), BF16),
             pltpu.VMEM((slots * LANES, slots * BLK), BF16),
             pltpu.VMEM((slots, 2 * LANES, LANES), BF16),
@@ -710,8 +726,8 @@
             pltpu.VMEM((lines, 2, rows, LANES), F32),
             dma((4, lines)),
             dma((4, lines)),
-            dma((2, 2)),
-            dma((2, 2)),
+            dma((2, 4)),
+            dma((2, 4)),
             dma((3, 8)),
             dma((3, 8)),
             dma((3, 2)),
@@ -722,7 +738,7 @@
         compiler_params=pltpu.CompilerParams(
             collective_id=1, has_side_effects=True, vmem_limit_bytes=48 * 2**20
         ),
-    )(ids, tensor, green)
+    )(*[jnp.transpose(x, (1, 2, 0)) for x in (source, occ, virt)], pairs.T, tensor, green)
 
 
 def solution(mesh):
@@ -743,7 +759,9 @@
         vmem = pl.BlockSpec(memory_space=pltpu.VMEM)
         dma = pltpu.SemaphoreType.DMA
         if n == 8 and groups % 2 == 0 and rows * 2 == BLK:
-            return on_line(n, groups, atoms, ids, tensor, green)
+            return on_line(
+                n, groups, atoms, source_slot, occupied_index, virtual_index, pair_index, tensor, green
+            )
         return pl.pallas_call(
             functools.partial(kernel, n, groups, atoms),
             out_shape=jax.ShapeDtypeStruct((rows, n * rows), F32),

time: 58.3 us -> 55.5 us (0.952)
  local copies, waits for them, and re-layouts: 5.81 us -> 2.64 us
  other arithmetic: 0.05 us -> 0.81 us
    unnamed x16 -> x10, local copies, waits for them, and re-layouts: 5.22 us -> 2.47 us
    concatenate x1, other arithmetic: 0.04 us -> 0.81 us  [shards(): jnp.concatenate([virtual_green, occupied_green], axis=0)]
where the time goes in v4:
time: 55.5 us; the launch traced here: 55.3 us
  Pallas kernels  51.7 us (93%)
  local copies, waits for them, and re-layouts  2.64 us (5%)
  other arithmetic  0.81 us (1%)
    pallas_call x1, Pallas kernels, on_line(): pl.pallas_call(functools.partial(line_kernel, n, groups, atoms), out_shap...  51.7 us
    unnamed x10, local copies, waits for them, and re-layouts  2.47 us

profile of v4, /device:TPU:0, one launch (start us, length us, event | category | flops | bytes accessed | tf_op | source)
XLA Modules:
  0.0 55.3 jit_solution(935272022423817768)
XLA Ops:
  0.0 0.8 %pad_maximum_fusion = bf16[8,4096]{1,0:T(8,128)(2,1)S(1)} fusion(bf16[4,4096]{1,0:T(4,128)(2,1)} %param.8, bf16[4,4096]{1,0:T(4,128)(2,1)} %param.9), kind=kLoop, calls=%fused_computation.1 | loop fusion | flops 131072 | bytes 131072 | tf_op jit(solution)/shard_map/concatenate | solution.py:755
  0.8 0.2 reshape.3.green_ref
  1.0 0.0 copy-start
  1.0 0.0 copy-start.1
  1.0 0.0 copy-start.2
  1.0 0.0 copy-start.3
  1.0 1.8 %copy.10 = bf16[32,4,4096]{2,0,1:T(8,128)(2,1)S(1)} copy(bf16[32,4,4096]{2,1,0:T(4,128)(2,1)} %param.7) | data formatting | bytes 2097152 | tf_op args[0]
  2.9 0.0 copy-done
  2.9 0.0 copy-done.1
  2.9 0.0 copy-done.2
  2.9 0.0 copy-done.3
  2.9 51.7 %shard_map.73 = f32[32,256]{1,0:T(8,128)S(1)} custom-call(s32[4,4,16]{2,1,0:T(4,128)S(1)} %bitcast.8, s32[4,4,16]{2,1,0:T(4,128)S(1)} %bitcast.9, s32[4,4,16]{2,1,0:T(4,128)S(1)} %bitcast.10, s32[4,16]{1,0:T(4,128)S(1)} %bitcast.11, bf16[4,32,4096]{2,1,0:T(8,128)(2,1)S(1)} %bitcast.7, bf16[8,64,64]{2,1,0:T(8,128)(2,1)S(1)} %reshape.3.green_ref), custom_call_target="tpu_custom_call" | custom-call | tf_op jit(solution)/shard_map/pallas_call | solution.py:701
  54.6 0.6 %copy.12 = f32[32,256]{1,0:T(8,128)} copy(f32[32,256]{1,0:T(8,128)S(1)} %shard_map.73) | data formatting | bytes 65536
Async XLA Ops:
  1.0 1.9 %copy-start = (s32[16,4,4]{0,2,1:T(4,128)S(1)}, s32[16,4,4]{0,2,1:T(4,128)}, u32[]{:S(2)}) copy-start(s32[16,4,4]{0,2,1:T(4,128)} %param.11) | copy-start | bytes 3076
  1.0 1.9 %copy-start.1 = (s32[16,4,4]{0,2,1:T(4,128)S(1)}, s32[16,4,4]{0,2,1:T(4,128)}, u32[]{:S(2)}) copy-start(s32[16,4,4]{0,2,1:T(4,128)} %param.12) | copy-start | bytes 3076
  1.0 1.9 %copy-start.2 = (s32[16,4,4]{0,2,1:T(4,128)S(1)}, s32[16,4,4]{0,2,1:T(4,128)}, u32[]{:S(2)}) copy-start(s32[16,4,4]{0,2,1:T(4,128)} %param.13) | copy-start | bytes 3076
  1.0 1.9 %copy-start.3 = (s32[16,4]{0,1:T(4,128)S(1)}, s32[16,4]{0,1:T(4,128)}, u32[]{:S(2)}) copy-start(s32[16,4]{0,1:T(4,128)} %param.10) | copy-start | bytes 772

commit v5 on v4

--- a/solution.py
+++ b/solution.py
@@ -316,19 +316,39 @@
         turned = nt(turned, perm).astype(BF16)
         table[mine + b] = jnp.concatenate([green_ref[b], turned], axis=1)
 
+    pl.semaphore_wait(barrier, n + 1)
+
+    def line(k):
+        return lax.rem(high + k, lines) * 2
+
+    def at_home(c):
+        return table.at[pl.ds(c * blocks, blocks)]
+
+    def across(c):
+        return table.at[pl.ds((n + c) * blocks, blocks)]
+
+    first_hop = [
+        remote(at_home(me), at_home(me), g_send.at[0, k], g_recv.at[0, k], dist, line(k) + low)
+        for k in range(1, lines)
+    ]
+    for copy in first_hop:
+        copy.start()
+    second_hop, third_hop = [], []
+
+    def onward(k):
+        c = line(lines - k) + low
+        second_hop.append(remote(at_home(c), at_home(c), g_send.at[1, k], g_recv.at[1, k], dist, partner))
+        second_hop[-1].start()
+        third_hop.append(remote(at_home(c), across(c), g_send.at[2, k], g_recv.at[2, k], before, me))
+        third_hop[-1].start()
+
+    onward(0)
+
     wide = slots * LANES
     r_, c_ = iota((wide, wide), 0), iota((wide, wide), 1)
     select[...] = (
         r_ == ((c_ // half) % slots) * LANES + ((c_ // LANES) % 2) * BLK + (c_ // (2 * LANES)) * half + c_ % half
     ).astype(BF16)
-    r_, c_ = iota((wide, slots * BLK), 0), iota((wide, slots * BLK), 1)
-    place[...] = ((r_ % LANES >= BLK) & (c_ == (r_ // LANES) * BLK + r_ % LANES - BLK)).astype(BF16)
-    r_, c_ = iota((2 * LANES, LANES), 0), iota((2 * LANES, LANES), 1)
-    for t in range(slots):
-        lift[t] = ((c_ < BLK) & (r_ == (c_ // half) * LANES + t * half + c_ % half)).astype(BF16)
-    r_, c_ = iota((LANES, wide), 0), iota((LANES, wide), 1)
-    turn_v[...] = ((r_ // half == c_ // LANES) & (c_ % LANES == low * half + r_ % half)).astype(BF16)
-
     own_rows = pl.ds(pl.multiple_of(low * rows, rows), rows)
     per = 8
     for q in range(0, chunks, per):
@@ -348,34 +368,6 @@
                         p * rows:(p + 1) * rows, (h * 2 + e) * LANES:(h * 2 + e + 1) * LANES
                     ]
 
-    pl.semaphore_wait(barrier, n + 1)
-
-    def line(k):
-        return lax.rem(high + k, lines) * 2
-
-    def at_home(c):
-        return table.at[pl.ds(c * blocks, blocks)]
-
-    def across(c):
-        return table.at[pl.ds((n + c) * blocks, blocks)]
-
-    first_hop = [
-        remote(at_home(me), at_home(me), g_send.at[0, k], g_recv.at[0, k], dist, line(k) + low)
-        for k in range(1, lines)
-    ]
-    for copy in first_hop:
-        copy.start()
-    second_hop, third_hop = [], []
-
-    def onward(k):
-        c = line(lines - k) + low
-        second_hop.append(remote(at_home(c), at_home(c), g_send.at[1, k], g_recv.at[1, k], dist, partner))
-        second_hop[-1].start()
-        third_hop.append(remote(at_home(c), across(c), g_send.at[2, k], g_recv.at[2, k], before, me))
-        third_hop[-1].start()
-
-    onward(0)
-
     def rows_of(k):
         y = low if k < 2 else 1 - low
         return pl.ds(pl.multiple_of(y * rows + (k % 2) * part_rows, part_rows), part_rows)
@@ -441,6 +433,14 @@
                 over_z(slot, k, x, False, a).wait_recv()
                 over_z(slot, k, x, False, a + 1).start()
 
+    r_, c_ = iota((wide, slots * BLK), 0), iota((wide, slots * BLK), 1)
+    place[...] = ((r_ % LANES >= BLK) & (c_ == (r_ // LANES) * BLK + r_ % LANES - BLK)).astype(BF16)
+    r_, c_ = iota((2 * LANES, LANES), 0), iota((2 * LANES, LANES), 1)
+    for t in range(slots):
+        lift[t] = ((c_ < BLK) & (r_ == (c_ // half) * LANES + t * half + c_ % half)).astype(BF16)
+    r_, c_ = iota((LANES, wide), 0), iota((LANES, wide), 1)
+    turn_v[...] = ((r_ // half == c_ // LANES) & (c_ % LANES == low * half + r_ % half)).astype(BF16)
+
     def third(k):
         second_hop[k].wait_recv()
         c = line(lines - k) + 1 - low
@@ -457,15 +457,6 @@
     relay(2, 1, 0)
     relay(2, 1, 1)
     relay(1, 0, 1)
-    spread(0)
-    spread(1)
-    relay(2, 1, 2)
-    relay(2, 0, 0)
-    for copy in third_hop:
-        copy.wait_recv()
-    for k in range(3):
-        send_own(k, (3,))
-
     total = n * blocks * groups
     base = dist * n * blocks
     atom = dist * lines + high
@@ -487,52 +478,32 @@
     def green(a, s, r, live):
         return position(occ_ids[s, r, a]), position(virt_ids[s, r, a]), live.astype(F32)
 
-    for t in range(slots):
-        virt = []
-        for o in range(slots):
-            r, live = feeding(atom, o, t)
-            occ_pos, virt_pos, live = green(atom, o, r, live)
-            virt.append((table[virt_pos].astype(F32) * live).astype(BF16))
-            gather[3, t * BLK:(t + 1) * BLK, o * LANES:(o + 1) * LANES] = table[occ_pos]
-        b = nt(turn_v[...], jnp.concatenate(virt, axis=1)).astype(BF16)
-        second_op[0, :, t * LANES:(t + 1) * LANES] = nt(lift[t][:, :BLK], b).astype(BF16)
-    size_op = slots * BLK
-    unit = (iota((size_op, size_op), 0) == iota((size_op, size_op), 1)).astype(BF16)
-    first_op[0] = nt(unit, nn(gather[3], place[...]).astype(BF16)).astype(BF16)
-
-    for x in range(pieces):
-        from_y(0, 1, x).wait_recv()
-    send_own(3, (0, 1, 3))
-
-    def operators(slot, a):
+    used = {0: (0, (1, 2, 3)), 1: (1, (2, 3)), 2: (3, (2,))}
+
+    def wanted_here(slot):
+        hit = place_at == used[slot][1][0]
+        for a in used[slot][1][1:]:
+            hit = hit | (place_at == a)
+        return hit
+
+    def adjoint_entries(a):
         other = atom_at(a)
+        entries = []
         for t in range(slots):
             pair = pair_ids[t, atom]
             s, met = jnp.int32(0), jnp.int32(0)
             for x in range(slots):
                 hit = pair_ids[x, other] == pair
                 s, met = jnp.where(hit, x, s), jnp.where(hit, 1, met)
-            virt = []
+            row = []
             for o in range(slots):
                 r, live = feeding(other, s, o)
-                occ_pos, virt_pos, live = green(other, s, r, live * met)
-                virt.append(
-                    (table[virt_pos, pl.ds(pl.multiple_of(low * half, half), half), :].astype(F32) * live).astype(BF16)
-                )
-                gather[slot, o * BLK:(o + 1) * BLK, t * LANES:(t + 1) * LANES] = table[occ_pos]
-            second_op[1 + slot, :, t * LANES:(t + 1) * LANES] = nt(lift[t], jnp.concatenate(virt, axis=0)).astype(BF16)
-        first_op[1 + slot] = nn(gather[slot], place[...]).astype(BF16)
-
-    used = {0: (0, (1, 2, 3)), 1: (1, (2, 3)), 2: (3, (2,))}
-
-    def wanted_here(slot):
-        hit = place_at == used[slot][1][0]
-        for a in used[slot][1][1:]:
-            hit = hit | (place_at == a)
-        return hit
-
-    for slot in used:
-        operators(slot, used[slot][0])
+                row.append(green(other, s, r, live * met))
+            entries.append(row)
+        return entries
+
+    own_entries = [[green(atom, o, *feeding(atom, o, t)) for o in range(slots)] for t in range(slots)]
+    entries = {slot: adjoint_entries(used[slot][0]) for slot in used}
 
     r_, c_ = iota((LANES, LANES), 0), iota((LANES, LANES), 1)
     for slot in used:
@@ -544,6 +515,46 @@
                 match = jnp.where((r_ // half == s) & (c_ // half == t), hit.astype(F32), match)
         match_op[:, slot * LANES:(slot + 1) * LANES] = jnp.where(r_ % half == c_ % half, match, 0.0).astype(BF16)
 
+    spread(0)
+    spread(1)
+    relay(2, 1, 2)
+    relay(2, 0, 0)
+    for copy in third_hop:
+        copy.wait_recv()
+    for k in range(3):
+        send_own(k, (3,))
+
+    for t in range(slots):
+        virt = []
+        for o in range(slots):
+            occ_pos, virt_pos, live = own_entries[t][o]
+            virt.append((table[virt_pos].astype(F32) * live).astype(BF16))
+            gather[3, t * BLK:(t + 1) * BLK, o * LANES:(o + 1) * LANES] = table[occ_pos]
+        b = nt(turn_v[...], jnp.concatenate(virt, axis=1)).astype(BF16)
+        second_op[0, :, t * LANES:(t + 1) * LANES] = nt(lift[t][:, :BLK], b).astype(BF16)
+    size_op = slots * BLK
+    unit = (iota((size_op, size_op), 0) == iota((size_op, size_op), 1)).astype(BF16)
+    first_op[0] = nt(unit, nn(gather[3], place[...]).astype(BF16)).astype(BF16)
+
+    for x in range(pieces):
+        from_y(0, 1, x).wait_recv()
+    send_own(3, (0, 1, 3))
+
+    def operators(slot):
+        for t in range(slots):
+            virt = []
+            for o in range(slots):
+                occ_pos, virt_pos, live = entries[slot][t][o]
+                virt.append(
+                    (table[virt_pos, pl.ds(pl.multiple_of(low * half, half), half), :].astype(F32) * live).astype(BF16)
+                )
+                gather[slot, o * BLK:(o + 1) * BLK, t * LANES:(t + 1) * LANES] = table[occ_pos]
+            second_op[1 + slot, :, t * LANES:(t + 1) * LANES] = nt(lift[t], jnp.concatenate(virt, axis=0)).astype(BF16)
+        first_op[1 + slot] = nn(gather[slot], place[...]).astype(BF16)
+
+    for slot in used:
+        operators(slot)
+
     lanes2 = (iota((BLK, 2 * LANES), 1) // half) % slots
 
     def first(k, u, g):
@@ -603,12 +614,16 @@
                         relay(a, slot, group)
 
         two_stacks(0, at_rows, g)
-        reorder(at_rows)
         relays(0)
 
         @pl.when(place_at >= 2)
         def _():
+            reorder(at_rows)
             two_stacks(2, at_rows, g)
+
+        @pl.when(place_at == 1)
+        def _():
+            reorder(at_rows)
         relays(1)
         return carry
 

time: 55.5 us -> 55.4 us (level)
  no operation moved by 1% of the time
where the time goes in v5:
time: 55.4 us; the launch traced here: 55.2 us
  Pallas kernels  51.7 us (93%)
  local copies, waits for them, and re-layouts  2.64 us (5%)
  other arithmetic  0.81 us (1%)
    pallas_call x1, Pallas kernels, on_line(): pl.pallas_call(functools.partial(line_kernel, n, groups, atoms), out_shap...  51.7 us
    unnamed x10, local copies, waits for them, and re-layouts  2.47 us

profile of v5, /device:TPU:0, one launch (start us, length us, event | category | flops | bytes accessed | tf_op | source)
XLA Modules:
  0.0 55.2 jit_solution(16020430229658266636)
XLA Ops:
  0.0 0.8 %pad_maximum_fusion = bf16[8,4096]{1,0:T(8,128)(2,1)S(1)} fusion(bf16[4,4096]{1,0:T(4,128)(2,1)} %param.8, bf16[4,4096]{1,0:T(4,128)(2,1)} %param.9), kind=kLoop, calls=%fused_computation.1 | loop fusion | flops 131072 | bytes 131072 | tf_op jit(solution)/shard_map/concatenate | solution.py:770
  0.8 0.2 reshape.3.green_ref
  1.0 0.0 copy-start
  1.0 0.0 copy-start.1
  1.0 0.0 copy-start.2
  1.0 0.0 copy-start.3
  1.0 1.8 %copy.10 = bf16[32,4,4096]{2,0,1:T(8,128)(2,1)S(1)} copy(bf16[32,4,4096]{2,1,0:T(4,128)(2,1)} %param.7) | data formatting | bytes 2097152 | tf_op args[0]
  2.9 0.0 copy-done
  2.9 0.0 copy-done.1
  2.9 0.0 copy-done.2
  2.9 0.0 copy-done.3
  2.9 51.7 %shard_map.73 = f32[32,256]{1,0:T(8,128)S(1)} custom-call(s32[4,4,16]{2,1,0:T(4,128)S(1)} %bitcast.8, s32[4,4,16]{2,1,0:T(4,128)S(1)} %bitcast.9, s32[4,4,16]{2,1,0:T(4,128)S(1)} %bitcast.10, s32[4,16]{1,0:T(4,128)S(1)} %bitcast.11, bf16[4,32,4096]{2,1,0:T(8,128)(2,1)S(1)} %bitcast.7, bf16[8,64,64]{2,1,0:T(8,128)(2,1)S(1)} %reshape.3.green_ref), custom_call_target="tpu_custom_call" | custom-call | tf_op jit(solution)/shard_map/pallas_call | solution.py:716
  54.6 0.6 %copy.12 = f32[32,256]{1,0:T(8,128)} copy(f32[32,256]{1,0:T(8,128)S(1)} %shard_map.73) | data formatting | bytes 65536
Async XLA Ops:
  1.0 1.9 %copy-start = (s32[16,4,4]{0,2,1:T(4,128)S(1)}, s32[16,4,4]{0,2,1:T(4,128)}, u32[]{:S(2)}) copy-start(s32[16,4,4]{0,2,1:T(4,128)} %param.11) | copy-start | bytes 3076
  1.0 1.9 %copy-start.1 = (s32[16,4,4]{0,2,1:T(4,128)S(1)}, s32[16,4,4]{0,2,1:T(4,128)}, u32[]{:S(2)}) copy-start(s32[16,4,4]{0,2,1:T(4,128)} %param.12) | copy-start | bytes 3076
  1.0 1.9 %copy-start.2 = (s32[16,4,4]{0,2,1:T(4,128)S(1)}, s32[16,4,4]{0,2,1:T(4,128)}, u32[]{:S(2)}) copy-start(s32[16,4,4]{0,2,1:T(4,128)} %param.13) | copy-start | bytes 3076
  1.0 1.9 %copy-start.3 = (s32[16,4]{0,1:T(4,128)S(1)}, s32[16,4]{0,1:T(4,128)}, u32[]{:S(2)}) copy-start(s32[16,4]{0,1:T(4,128)} %param.10) | copy-start | bytes 772

commit v6 on v5

--- a/solution.py
+++ b/solution.py
@@ -661,7 +661,7 @@
             returned(slot, y).start()
         blk[flip(a)] = both[BLK:]
 
-    for slot in (2, 1, 0):
+    for slot in (1, 0, 2):
         @pl.when(wanted_here(slot))
         def _():
             product(slot)

time: 55.4 us -> 55 us (level)
  no operation moved by 1% of the time
where the time goes in v6:
time: 55 us; the launch traced here: 54.8 us
  Pallas kernels  51.3 us (93%)
  local copies, waits for them, and re-layouts  2.64 us (5%)
  other arithmetic  0.81 us (1%)
    pallas_call x1, Pallas kernels, on_line(): pl.pallas_call(functools.partial(line_kernel, n, groups, atoms), out_shap...  51.3 us
    unnamed x10, local copies, waits for them, and re-layouts  2.47 us

profile of v6, /device:TPU:0, one launch (start us, length us, event | category | flops | bytes accessed | tf_op | source)
XLA Modules:
  0.0 54.8 jit_solution(6195247088760841468)
XLA Ops:
  0.0 0.8 %pad_maximum_fusion = bf16[8,4096]{1,0:T(8,128)(2,1)S(1)} fusion(bf16[4,4096]{1,0:T(4,128)(2,1)} %param.8, bf16[4,4096]{1,0:T(4,128)(2,1)} %param.9), kind=kLoop, calls=%fused_computation.1 | loop fusion | flops 131072 | bytes 131072 | tf_op jit(solution)/shard_map/concatenate | solution.py:770
  0.8 0.2 reshape.3.green_ref
  1.0 0.0 copy-start
  1.0 0.0 copy-start.1
  1.0 0.0 copy-start.2
  1.0 0.0 copy-start.3
  1.0 1.8 %copy.10 = bf16[32,4,4096]{2,0,1:T(8,128)(2,1)S(1)} copy(bf16[32,4,4096]{2,1,0:T(4,128)(2,1)} %param.7) | data formatting | bytes 2097152 | tf_op args[0]
  2.9 0.0 copy-done
  2.9 0.0 copy-done.1
  2.9 0.0 copy-done.2
  2.9 0.0 copy-done.3
  2.9 51.3 %shard_map.73 = f32[32,256]{1,0:T(8,128)S(1)} custom-call(s32[4,4,16]{2,1,0:T(4,128)S(1)} %bitcast.8, s32[4,4,16]{2,1,0:T(4,128)S(1)} %bitcast.9, s32[4,4,16]{2,1,0:T(4,128)S(1)} %bitcast.10, s32[4,16]{1,0:T(4,128)S(1)} %bitcast.11, bf16[4,32,4096]{2,1,0:T(8,128)(2,1)S(1)} %bitcast.7, bf16[8,64,64]{2,1,0:T(8,128)(2,1)S(1)} %reshape.3.green_ref), custom_call_target="tpu_custom_call" | custom-call | tf_op jit(solution)/shard_map/pallas_call | solution.py:716
  54.2 0.6 %copy.12 = f32[32,256]{1,0:T(8,128)} copy(f32[32,256]{1,0:T(8,128)S(1)} %shard_map.73) | data formatting | bytes 65536
Async XLA Ops:
  1.0 1.9 %copy-start = (s32[16,4,4]{0,2,1:T(4,128)S(1)}, s32[16,4,4]{0,2,1:T(4,128)}, u32[]{:S(2)}) copy-start(s32[16,4,4]{0,2,1:T(4,128)} %param.11) | copy-start | bytes 3076
  1.0 1.9 %copy-start.1 = (s32[16,4,4]{0,2,1:T(4,128)S(1)}, s32[16,4,4]{0,2,1:T(4,128)}, u32[]{:S(2)}) copy-start(s32[16,4,4]{0,2,1:T(4,128)} %param.12) | copy-start | bytes 3076
  1.0 1.9 %copy-start.2 = (s32[16,4,4]{0,2,1:T(4,128)S(1)}, s32[16,4,4]{0,2,1:T(4,128)}, u32[]{:S(2)}) copy-start(s32[16,4,4]{0,2,1:T(4,128)} %param.13) | copy-start | bytes 3076
  1.0 1.9 %copy-start.3 = (s32[16,4]{0,1:T(4,128)S(1)}, s32[16,4]{0,1:T(4,128)}, u32[]{:S(2)}) copy-start(s32[16,4]{0,1:T(4,128)} %param.10) | copy-start | bytes 772

commit v7 on v6

--- a/solution.py
+++ b/solution.py
@@ -661,8 +661,8 @@
             returned(slot, y).start()
         blk[flip(a)] = both[BLK:]
 
-    for slot in (1, 0, 2):
-        @pl.when(wanted_here(slot))
+    for slot, a in ((1, 3), (0, 1), (0, 2), (0, 3), (2, 2), (1, 2)):
+        @pl.when(place_at == a)
         def _():
             product(slot)
 

time: 55 us -> 55 us (level)
  no operation moved by 1% of the time
where the time goes in v7:
time: 55 us; the launch traced here: 54.8 us
  Pallas kernels  51.3 us (93%)
  local copies, waits for them, and re-layouts  2.64 us (5%)
  other arithmetic  0.81 us (1%)
    pallas_call x1, Pallas kernels, on_line(): pl.pallas_call(functools.partial(line_kernel, n, groups, atoms), out_shap...  51.3 us
    unnamed x10, local copies, waits for them, and re-layouts  2.47 us

profile of v7, /device:TPU:0, one launch (start us, length us, event | category | flops | bytes accessed | tf_op | source)
XLA Modules:
  0.0 54.8 jit_solution(10835490990940477432)
XLA Ops:
  0.0 0.8 %pad_maximum_fusion = bf16[8,4096]{1,0:T(8,128)(2,1)S(1)} fusion(bf16[4,4096]{1,0:T(4,128)(2,1)} %param.8, bf16[4,4096]{1,0:T(4,128)(2,1)} %param.9), kind=kLoop, calls=%fused_computation.1 | loop fusion | flops 131072 | bytes 131072 | tf_op jit(solution)/shard_map/concatenate | solution.py:770
  0.8 0.2 reshape.3.green_ref
  1.0 0.0 copy-start
  1.0 0.0 copy-start.1
  1.0 0.0 copy-start.2
  1.0 0.0 copy-start.3
  1.0 1.8 %copy.10 = bf16[32,4,4096]{2,0,1:T(8,128)(2,1)S(1)} copy(bf16[32,4,4096]{2,1,0:T(4,128)(2,1)} %param.7) | data formatting | bytes 2097152 | tf_op args[0]
  2.9 0.0 copy-done
  2.9 0.0 copy-done.1
  2.9 0.0 copy-done.2
  2.9 0.0 copy-done.3
  2.9 51.3 %shard_map.73 = f32[32,256]{1,0:T(8,128)S(1)} custom-call(s32[4,4,16]{2,1,0:T(4,128)S(1)} %bitcast.8, s32[4,4,16]{2,1,0:T(4,128)S(1)} %bitcast.9, s32[4,4,16]{2,1,0:T(4,128)S(1)} %bitcast.10, s32[4,16]{1,0:T(4,128)S(1)} %bitcast.11, bf16[4,32,4096]{2,1,0:T(8,128)(2,1)S(1)} %bitcast.7, bf16[8,64,64]{2,1,0:T(8,128)(2,1)S(1)} %reshape.3.green_ref), custom_call_target="tpu_custom_call" | custom-call | tf_op jit(solution)/shard_map/pallas_call | solution.py:716
  54.2 0.6 %copy.12 = f32[32,256]{1,0:T(8,128)} copy(f32[32,256]{1,0:T(8,128)S(1)} %shard_map.73) | data formatting | bytes 65536
Async XLA Ops:
  1.0 1.9 %copy-start = (s32[16,4,4]{0,2,1:T(4,128)S(1)}, s32[16,4,4]{0,2,1:T(4,128)}, u32[]{:S(2)}) copy-start(s32[16,4,4]{0,2,1:T(4,128)} %param.11) | copy-start | bytes 3076
  1.0 1.9 %copy-start.1 = (s32[16,4,4]{0,2,1:T(4,128)S(1)}, s32[16,4,4]{0,2,1:T(4,128)}, u32[]{:S(2)}) copy-start(s32[16,4,4]{0,2,1:T(4,128)} %param.12) | copy-start | bytes 3076
  1.0 1.9 %copy-start.2 = (s32[16,4,4]{0,2,1:T(4,128)S(1)}, s32[16,4,4]{0,2,1:T(4,128)}, u32[]{:S(2)}) copy-start(s32[16,4,4]{0,2,1:T(4,128)} %param.13) | copy-start | bytes 3076
  1.0 1.9 %copy-start.3 = (s32[16,4]{0,1:T(4,128)S(1)}, s32[16,4]{0,1:T(4,128)}, u32[]{:S(2)}) copy-start(s32[16,4]{0,1:T(4,128)} %param.10) | copy-start | bytes 772
